TPU v7x, 128 devices: a whole 4x4x4 slice. The times are simulated.
128 devices in a mesh: list: 8 (over y, core), shard: 16 (over x, z).
Axes of the slice: x: 4, y: 4, z: 4, core: 2. Of those that a mesh axis runs over, the one named last changes fastest.
Arguments:
- embeddings: bfloat16 [262144, 768], P(('list', 'shard')), may hold values from -6 to 6
- list_ids: int32 [262144, 1], P(('list', 'shard')), may hold values from 0 to 15; in each aligned block of 2048 rows (0 to 2047, 2048 to 4095, ...) at most 256 rows name the same one
- centroids: bfloat16 [16, 1024, 768], P('list'), may hold values from -6 to 6
Outputs:
- new_centroids: float32 [16, 1024, 768], P('list', 'shard')
Inputs may be any that keep to these rules, and one draw needn't show every extreme that they name: `list_ids`: within each device's 2048 rows no coarse list is named by more than 256 rows, a bound that some block reaches.
All inputs are finite; a program needn't handle non-finite values.
Results may differ from a plain program's by a relative error of at most 0.0014.
Values may be sent and summed in bfloat16 or wider, within the bound.
No kernel may reach another device: no remote copies, remote signals or barrier semaphores. Data moves between devices by JAX's collectives and lax.ppermute only.
A program may use at most 64 MiB of HBM per device.

v0:
```python
import functools
import math

import jax
import jax.numpy as jnp
import numpy as np
from jax import lax
from jax.experimental import pallas as pl
from jax.experimental.pallas import tpu as pltpu
from jax.sharding import PartitionSpec as P

SHARP = 0.1
PRIOR = 1.0
LOG2E = math.log2(math.e)
LANES = 128
PAD_MARK = 64.0
PAD_TEST = 32.0
TAIL_ROWS = 16
PIECES = 4
HOPS = ((1, 0), (3, 0), (1, 1), (3, 1), (2, 0), (2, 1), (0, 1), (0, 0))
STAGES = (((7, 0, 1), (2, 3, 6), (4, 5)), ((7, 0, 1, 2, 3), (4, 5, 6)))
TIED = 4
FIRST = 2
VMEM = pl.BlockSpec(memory_space=pltpu.VMEM)
SMEM = pl.BlockSpec(memory_space=pltpu.SMEM)
PARAMS = pltpu.CompilerParams(vmem_limit_bytes=20 * 2**20)


def count_into(key_ref, count_ref, ids_ref):
    lists = key_ref.shape[0]
    names = lax.broadcasted_iota(jnp.int32, (lists, LANES), 0)
    earlier = lax.broadcasted_iota(jnp.int32, (LANES, LANES), 0) < lax.broadcasted_iota(jnp.int32, (LANES, LANES), 1)
    earlier = jnp.where(earlier, 1.0, 0.0).astype(jnp.bfloat16)
    seen = jnp.zeros((lists, 1), jnp.float32)
    for b in range(ids_ref.shape[1] // LANES):
        hit = ids_ref[:, b * LANES : (b + 1) * LANES] == names
        hot = jnp.where(hit, 1.0, 0.0)
        before = jnp.dot(hot.astype(jnp.bfloat16), earlier, preferred_element_type=jnp.float32) + seen
        key_ref[:, b * LANES : (b + 1) * LANES] = jnp.where(hit, before, -1.0).astype(jnp.int32)
        seen = seen + jnp.sum(hot, axis=1, keepdims=True)
    count_ref[...] = jnp.broadcast_to(seen, count_ref.shape).astype(jnp.int32)


def pack_kernel(first, at, *refs):
    if first:
        names_ref, ids_ref, rows_ref, key_ref, count_ref, *outs = refs
        count_into(key_ref, count_ref, ids_ref)
    else:
        names_ref, rows_ref, key_ref, count_ref, *outs = refs
    cap = outs[0].shape[0]
    slots = lax.broadcasted_iota(jnp.int32, (cap, rows_ref.shape[0]), 0)
    lane = lax.broadcasted_iota(jnp.int32, (cap, LANES), 1)
    slot = lax.broadcasted_iota(jnp.int32, (cap, LANES), 0)
    for k, out_ref in enumerate(outs):
        name = names_ref[at + k]
        pick = jnp.where(key_ref[pl.ds(name, 1), :] == slots, 1.0, 0.0).astype(jnp.bfloat16)
        out = jnp.dot(pick, rows_ref[...], preferred_element_type=jnp.float32)
        out_ref[...] = out.astype(jnp.bfloat16)
        padding = (lane == 0) & (slot >= count_ref[pl.ds(name, 1), :])
        out_ref[:, :LANES] = jnp.where(padding, PAD_MARK, out[:, :LANES]).astype(jnp.bfloat16)


def pack(names, at, blocks, rows, lists, cap, ids=None, keys=None):
    count, width = rows.shape
    made = [jax.ShapeDtypeStruct((cap, width), jnp.bfloat16)] * blocks
    kept = [jax.ShapeDtypeStruct((lists, count), jnp.int32), jax.ShapeDtypeStruct((lists, LANES), jnp.int32)]
    operands = [names] + ([ids, rows] if keys is None else [rows, *keys])
    made = (kept if keys is None else []) + made
    out = pl.pallas_call(
        functools.partial(pack_kernel, keys is None, at),
        out_shape=made,
        in_specs=[SMEM] + [VMEM] * (len(operands) - 1),
        out_specs=[VMEM] * len(made),
        compiler_params=PARAMS,
        cost_estimate=pl.CostEstimate(
            flops=2 * blocks * cap * count * width, bytes_accessed=2 * rows.size, transcendentals=0
        ),
        name="pack",
    )(*operands)
    out = list(out)
    return (out[:2], out[2:]) if keys is None else out


def norm_kernel(cents_ref, *outs):
    for index, out_ref in enumerate(outs):
        c = cents_ref[index].astype(jnp.float32)
        total = jnp.sum(jnp.square(c), axis=1, keepdims=True) * (0.5 * SHARP * LOG2E)
        out_ref[...] = jnp.broadcast_to(total, out_ref.shape)


def norms(cents):
    local, fine, _ = cents.shape
    return pl.pallas_call(
        norm_kernel,
        out_shape=[jax.ShapeDtypeStruct((fine, LANES), jnp.float32)] * local,
        in_specs=[VMEM],
        out_specs=[VMEM] * local,
        compiler_params=PARAMS,
        name="norms",
    )(cents)


def raw_scores(cents_ref, index, rows_ref):
    return lax.dot_general(
        cents_ref[index], rows_ref[...], (((1,), (1,)), ((), ())), preferred_element_type=jnp.float32
    )


def responses(raw, norm_ref, rows_ref):
    cap = rows_ref.shape[0]
    norm = jnp.concatenate([norm_ref[...]] * (cap // LANES), axis=1)
    scores = raw * (SHARP * LOG2E) - norm
    p = jnp.exp2(scores - jnp.max(scores, axis=0, keepdims=True))
    mark = jnp.transpose(rows_ref[:, :LANES].astype(jnp.float32))[0:1, :]
    scale = jnp.where(mark < PAD_TEST, 1.0, 0.0) / jnp.sum(p, axis=0, keepdims=True)
    resp = (p * scale).astype(jnp.bfloat16)
    back = resp.astype(jnp.float32)
    mass = back[:, :LANES]
    for j in range(1, cap // LANES):
        mass = mass + back[:, j * LANES : (j + 1) * LANES]
    return resp, mass


def respond(cents_ref, index, norm_ref, row_refs, all_ref, resp_ref, total):
    raw = raw_scores(cents_ref, index, row_refs[0])
    for n, rows_ref in enumerate(row_refs):
        cap = rows_ref.shape[0]
        now = raw
        if n + 1 < len(row_refs):
            raw = raw_scores(cents_ref, index, row_refs[n + 1])
        all_ref[n * cap : (n + 1) * cap, :] = rows_ref[...]
        resp, mass = responses(now, norm_ref, rows_ref)
        resp_ref[:, n * cap : (n + 1) * cap] = resp
        total = mass if total is None else total + mass
    return total


def stats_kernel(index, blocks, carried, *refs):
    cents_ref, norm_ref = refs[:2]
    row_refs = refs[2 : 2 + blocks]
    sums_ref, mass_ref, all_ref, resp_ref = refs[-4:]
    old = refs[3 + blocks][...] if carried else None
    mass_ref[...] = respond(cents_ref, index, norm_ref, row_refs, all_ref, resp_ref, old)
    size = sums_ref.shape[0] // PIECES
    for at in range(0, sums_ref.shape[0], size):
        part = jnp.dot(resp_ref[at : at + size, :], all_ref[...], preferred_element_type=jnp.float32)
        if carried:
            part = refs[2 + blocks][at : at + size, :] + part
        sums_ref[at : at + size, :] = part


def last_kernel(index, blocks, shares, *refs):
    cents_ref, norm_ref = refs[:2]
    row_refs = refs[2 : 2 + blocks]
    sums_ref, mass_ref, out_ref, old_ref, send_ref, all_ref, resp_ref, in_sem, out_sem = refs[2 + blocks :]
    load = pltpu.make_async_copy(sums_ref, old_ref, in_sem)
    load.start()
    fine, width = old_ref.shape
    share = fine // shares
    groups = width // LANES
    total = respond(cents_ref, index, norm_ref, row_refs, all_ref, resp_ref, mass_ref[...])
    line = jnp.sum(jnp.transpose(total), axis=0, keepdims=True)
    high = line.astype(jnp.bfloat16).astype(jnp.float32)
    low = line - high
    row = lax.broadcasted_iota(jnp.int32, (TAIL_ROWS, LANES), 0)
    load.wait()
    copies = []
    per = shares // PIECES
    for piece in range(PIECES):
        at = piece * per * share
        part = jnp.dot(resp_ref[at : at + per * share, :], all_ref[...], preferred_element_type=jnp.float32)
        part = old_ref[at : at + per * share, :] + part
        for t in range(per):
            s = piece * per + t
            for j in range(groups):
                some = part[t * share : (t + 1) * share, j * LANES : (j + 1) * LANES]
                send_ref[s, j * share : (j + 1) * share, :] = some.astype(jnp.bfloat16)
            where = s * share // LANES * LANES
            both = jnp.where(row == 0, high[:, where : where + LANES], jnp.where(row == 1, low[:, where : where + LANES], 0.0))
            send_ref[s, groups * share :, :] = both.astype(jnp.bfloat16)
        rng = pl.ds(piece * per, per)
        copies.append(pltpu.make_async_copy(send_ref.at[rng], out_ref.at[rng], out_sem.at[piece]))
        copies[-1].start()
    for copy in copies:
        copy.wait()


def stats(cents, index, norm, rows, carried):
    _, fine, width = cents.shape
    sums = jax.ShapeDtypeStruct((fine, width), jnp.float32)
    mass = jax.ShapeDtypeStruct((fine, LANES), jnp.float32)
    count = sum(r.shape[0] for r in rows)
    operands = [cents, norm, *rows, *(carried or ())]
    return pl.pallas_call(
        functools.partial(stats_kernel, index, len(rows), carried is not None),
        out_shape=[sums, mass],
        in_specs=[VMEM] * len(operands),
        out_specs=[VMEM, VMEM],
        scratch_shapes=[pltpu.VMEM((count, width), jnp.bfloat16), pltpu.VMEM((fine, count), jnp.bfloat16)],
        compiler_params=PARAMS,
        name=f"stats_{index}",
    )(*operands)


def last_stats(cents, index, norm, rows, carried, shares):
    _, fine, width = cents.shape
    sent = (shares, fine // shares * (width // LANES) + TAIL_ROWS, LANES)
    count = sum(r.shape[0] for r in rows)
    operands = [cents, norm, *rows, *carried]
    return pl.pallas_call(
        functools.partial(last_kernel, index, len(rows), shares),
        out_shape=jax.ShapeDtypeStruct(sent, jnp.bfloat16),
        in_specs=[VMEM] * (2 + len(rows)) + [pl.BlockSpec(memory_space=pl.ANY), VMEM],
        out_specs=pl.BlockSpec(memory_space=pltpu.HBM),
        scratch_shapes=[
            pltpu.VMEM((fine, width), jnp.float32),
            pltpu.VMEM(sent, jnp.bfloat16),
            pltpu.VMEM((count, width), jnp.bfloat16),
            pltpu.VMEM((fine, count), jnp.bfloat16),
            pltpu.SemaphoreType.DMA,
            pltpu.SemaphoreType.DMA((PIECES,)),
        ],
        compiler_params=PARAMS,
        name=f"last_{index}",
    )(*operands)


def finish_kernel(index, shares, me_ref, got_ref, cents_ref, *rest):
    out_ref, load_ref, own_ref, made_ref, mass_ref, load_sem, own_sem, out_sem = rest[-8:]
    share, width = made_ref.shape
    groups = width // LANES
    ranges = [(groups * share, TAIL_ROWS)] + [(j * share, share) for j in range(groups)]
    loads = []
    for n, (at, size) in enumerate(ranges):
        rng = pl.ds(at, size)
        loads.append(pltpu.make_async_copy(got_ref.at[:, rng, :], load_ref.at[:, rng, :], load_sem.at[n]))
        loads[-1].start()
    first = pl.multiple_of(me_ref[0] * share, share)
    mine = pltpu.make_async_copy(cents_ref.at[index, pl.ds(first, share), :], own_ref, own_sem)
    mine.start()
    loads[0].wait()
    at = groups * share
    tail = load_ref[0, at : at + TAIL_ROWS, :].astype(jnp.float32)
    for k in range(1, shares):
        tail = tail + load_ref[k, at : at + TAIL_ROWS, :].astype(jnp.float32)
    mass_ref[...] = jnp.transpose(jnp.broadcast_to(tail[0:1, :] + tail[1:2, :], (LANES, LANES)))
    offset = pl.multiple_of(lax.rem(me_ref[0] * share, LANES), share)
    scale = 1.0 / (mass_ref[pl.ds(offset, share), :] + PRIOR)
    mine.wait()
    for j in range(groups):
        loads[1 + j].wait()
        at = j * share
        total = PRIOR * own_ref[:, j * LANES : (j + 1) * LANES].astype(jnp.float32)
        for k in range(shares):
            total = total + load_ref[k, at : at + share, :].astype(jnp.float32)
        made_ref[:, j * LANES : (j + 1) * LANES] = total * scale
    store = pltpu.make_async_copy(made_ref, out_ref.at[index], out_sem)
    store.start()
    store.wait()


def finish(me, got, cents, index, sofar):
    local, fine, width = cents.shape
    shares = got.shape[0]
    share = fine // shares
    anywhere = pl.BlockSpec(memory_space=pl.ANY)
    operands = [me, got, cents] + ([] if sofar is None else [sofar])
    return pl.pallas_call(
        functools.partial(finish_kernel, index, shares),
        out_shape=jax.ShapeDtypeStruct((local, share, width), jnp.float32),
        in_specs=[SMEM] + [anywhere] * (len(operands) - 1),
        out_specs=pl.BlockSpec(memory_space=pltpu.HBM),
        scratch_shapes=[
            pltpu.VMEM(got.shape, jnp.bfloat16),
            pltpu.VMEM((share, width), jnp.bfloat16),
            pltpu.VMEM((share, width), jnp.float32),
            pltpu.VMEM((LANES, LANES), jnp.float32),
            pltpu.SemaphoreType.DMA((1 + width // LANES,)),
            pltpu.SemaphoreType.DMA,
            pltpu.SemaphoreType.DMA,
        ],
        input_output_aliases={} if sofar is None else {3: 0},
        compiler_params=PARAMS,
        name=f"finish_{index}",
    )(*operands)


def target(g, step, groups):
    return (g // 2 + step[0]) % (groups // 2) * 2 + (g % 2 ^ step[1])


def hop(block, step, groups):
    if step == (0, 0):
        return block
    return lax.ppermute(block, "list", [(g, target(g, step, groups)) for g in range(groups)])


def per_device(embeddings, list_ids, centroids):
    groups = lax.axis_size("list")
    shares = lax.axis_size("shard")
    local = centroids.shape[0]
    lists = local * groups
    cap = embeddings.shape[0] // 8
    ids = list_ids.reshape(1, -1)
    g = lax.axis_index("list").astype(jnp.int32)
    me = lax.axis_index("shard").astype(jnp.int32).reshape(1)
    table = [[target(k, step, groups) for step in HOPS] for k in range(groups)]
    table = np.array([[d * local + i for i in range(local) for d in row] for row in table], np.int32)
    names = lax.dynamic_index_in_dim(jnp.asarray(table), g, 0, keepdims=False)
    tie = lax.optimization_barrier
    keys, sent = pack(names, 0, FIRST, embeddings, lists, cap, ids=ids)
    sent = sent + pack(names, FIRST, groups - FIRST, embeddings, lists, cap, keys=keys)
    later = []
    for at in range(0, groups, TIED):
        later += pack(names, groups + at, TIED, embeddings, lists, cap, keys=keys)
    sent[-1], later = tie((sent[-1], later))
    norm = norms(centroids)
    rows = [[hop(b, step, groups) for b, step in zip(blocks, HOPS)] for blocks in (sent, later)]
    out, got = None, []
    for index in range(local):
        stages = STAGES[index]
        carried = None
        for stage in stages[:-1]:
            carried = stats(centroids, index, norm[index], [rows[index][k] for k in stage], carried)
        part = last_stats(centroids, index, norm[index], [rows[index][k] for k in stages[-1]], carried, shares)
        if index == 0:
            part, rows[1][:TIED] = tie((part, rows[1][:TIED]))
        else:
            out = finish(me, got[0], centroids, 0, None)
        got.append(lax.all_to_all(part, "shard", split_axis=0, concat_axis=0, tiled=True))
    return finish(me, got[1], centroids, 1, out)


def solution(mesh):
    placed = (P(("list", "shard"), None), P(("list", "shard"), None), P("list", None, None))
    return jax.shard_map(
        per_device, mesh=mesh, in_specs=placed, out_specs=P("list", "shard", None), check_vma=False
    )
```

profile of v0, /device:TPU:1, one launch (start us, length us, event | category | flops | bytes accessed | tf_op | source)
XLA Modules:
  0.0 133.4 jit_solution(14250225868685303183)
XLA Ops:
  0.0 0.7 dynamic-slice_bitcast_fusion.refs_0_
  0.7 1.9 %copy-done.14 = bf16[2048,768]{1,0:T(8,128)(2,1)S(1)} copy-done((bf16[2048,768]{1,0:T(8,128)(2,1)S(1)}, bf16[2048,768]{1,0:T(8,128)(2,1)}, u32[]{:S(2)}) %copy-start.14) | copy-done | bytes 3145752
  2.6 0.7 copy-done.19
  3.3 2.6 %pack.4 = (s32[16,2048]{1,0:T(8,128)S(1)}, s32[16,128]{1,0:T(8,128)S(1)}, bf16[256,768]{1,0:T(8,128)(2,1)S(1)}, bf16[256,768]{1,0:T(8,128)(2,1)S(1)}) custom-call(s32[16]{0:T(128)S(1)} %dynamic-slice_bitcast_fusion.refs_0_, s32[1,2048]{1,0:T(1,128)S(1)} %bitcast.4, bf16[2048,768]{1,0:T(8,128)(2,1)S(1)} %copy-done.14), custom_call_target="tpu_custom_call" | custom-call | flops 1610612736 | bytes 3145728 | tf_op jit(solution)/shard_map/pack/pallas_call | solution.py:69
  5.8 2.2 %collective-permute-start.8 = (bf16[256,768]{1,0:T(8,128)(2,1)S(1)}, bf16[256,768]{1,0:T(8,128)(2,1)S(1)}, u32[]{:S(2)}, u32[]{:S(2)}) collective-permute-start(bf16[256,768]{1,0:T(8,128)(2,1)S(1)} %get-tuple-element.68), channel_id=1, source_target_pairs={{0,32},{16,48},{32,64},{48,80},{64,96},{80,112},{96,0},{112,16},{1... | collective-permute-start | bytes 1179656 | tf_op jit(solution)/shard_map/ppermute | solution.py:295
  8.0 1.5 %collective-permute-start.9 = (bf16[256,768]{1,0:T(8,128)(2,1)S(1)}, bf16[256,768]{1,0:T(8,128)(2,1)S(1)}, u32[]{:S(2)}, u32[]{:S(2)}) collective-permute-start(bf16[256,768]{1,0:T(8,128)(2,1)S(1)} %get-tuple-element.69), channel_id=1, source_target_pairs={{0,96},{16,112},{32,0},{48,16},{64,32},{80,48},{96,64},{112,80},{1... | collective-permute-start | bytes 1179656 | tf_op jit(solution)/shard_map/ppermute | solution.py:295
  9.6 5.6 %pack.5 = (bf16[256,768]{1,0:T(8,128)(2,1)S(1)}, bf16[256,768]{1,0:T(8,128)(2,1)S(1)}, bf16[256,768]{1,0:T(8,128)(2,1)S(1)}, bf16[256,768]{1,0:T(8,128)(2,1)S(1)...) custom-call(s32[16]{0:T(128)S(1)} %dynamic-slice_bitcast_fusion.refs_0_, bf16[2048,768]{1,0:T(8,128)(2,1)S(1)} %copy-done.14, ...), custom_call_target="tpu_custom_call" | custom-call | flops 4831838208 | bytes 3145728 | tf_op jit(solution)/shard_map/pack/pallas_call | solution.py:69
  15.1 1.6 %collective-permute-start.3 = (bf16[256,768]{1,0:T(8,128)(2,1)S(1)}, bf16[256,768]{1,0:T(8,128)(2,1)S(1)}, u32[]{:S(2)}, u32[]{:S(2)}) collective-permute-start(bf16[256,768]{1,0:T(8,128)(2,1)S(1)} %get-tuple-element.62), channel_id=1, source_target_pairs={{0,64},{16,80},{32,96},{48,112},{64,0},{80,16},{96,32},{112,48},{1... | collective-permute-start | bytes 1179656 | tf_op jit(solution)/shard_map/ppermute | solution.py:295
  16.8 1.8 %collective-permute-start.5 = (bf16[256,768]{1,0:T(8,128)(2,1)S(1)}, bf16[256,768]{1,0:T(8,128)(2,1)S(1)}, u32[]{:S(2)}, u32[]{:S(2)}) collective-permute-start(bf16[256,768]{1,0:T(8,128)(2,1)S(1)} %get-tuple-element.64), channel_id=1, source_target_pairs={{0,48},{16,32},{32,80},{48,64},{64,112},{80,96},{96,16},{112,0},{1... | collective-permute-start | bytes 1179656 | tf_op jit(solution)/shard_map/ppermute | solution.py:295
  18.6 1.2 collective-permute-start.6
  19.7 0.0 collective-permute-done.8.refs_3_
  19.8 1.5 %collective-permute-start.7 = (bf16[256,768]{1,0:T(8,128)(2,1)S(1)}, bf16[256,768]{1,0:T(8,128)(2,1)S(1)}, u32[]{:S(2)}, u32[]{:S(2)}) collective-permute-start(bf16[256,768]{1,0:T(8,128)(2,1)S(1)} %get-tuple-element.66), channel_id=1, source_target_pairs={{0,16},{16,0},{32,48},{48,32},{64,80},{80,64},{96,112},{112,96},{1... | collective-permute-start | bytes 1179656 | tf_op jit(solution)/shard_map/ppermute | solution.py:295
  21.3 4.0 %pack.7 = (bf16[256,768]{1,0:T(8,128)(2,1)S(1)}, bf16[256,768]{1,0:T(8,128)(2,1)S(1)}, bf16[256,768]{1,0:T(8,128)(2,1)S(1)}, bf16[256,768]{1,0:T(8,128)(2,1)S(1)}) custom-call(s32[16]{0:T(128)S(1)} %dynamic-slice_bitcast_fusion.refs_0_, bf16[2048,768]{1,0:T(8,128)(2,1)S(1)} %copy-done.14, s32[16,2048]{1,0:T(8,128)S(1)} %get-tuple-element.46.refs_2_, ...), custom_call_target="tpu_custom_call" | custom-call | flops 3221225472 | bytes 3145728 | tf_op jit(solution)/shard_map/pack/pallas_call | solution.py:69
  25.2 0.0 copy-start.16
  25.2 0.7 copy-done.16
  26.0 0.8 copy-done.17
  26.7 0.7 copy-done.18
  27.5 4.0 %pack.6 = (bf16[256,768]{1,0:T(8,128)(2,1)S(1)}, bf16[256,768]{1,0:T(8,128)(2,1)S(1)}, bf16[256,768]{1,0:T(8,128)(2,1)S(1)}, bf16[256,768]{1,0:T(8,128)(2,1)S(1)}) custom-call(s32[16]{0:T(128)S(1)} %dynamic-slice_bitcast_fusion.refs_0_, bf16[2048,768]{1,0:T(8,128)(2,1)S(1)} %copy-done.15, s32[16,2048]{1,0:T(8,128)S(1)} %get-tuple-element.46.refs_2_, ...), custom_call_target="tpu_custom_call" | custom-call | flops 3221225472 | bytes 3145728 | tf_op jit(solution)/shard_map/pack/pallas_call | solution.py:69
  31.4 0.0 collective-permute-done.9.refs_4_
  31.4 0.1 collective-permute-start.10
  31.5 0.0 collective-permute-done.3.refs_2_
  31.5 1.9 %collective-permute-start.4 = (bf16[256,768]{1,0:T(8,128)(2,1)S(1)}, bf16[256,768]{1,0:T(8,128)(2,1)S(1)}, u32[]{:S(2)}, u32[]{:S(2)}) collective-permute-start(bf16[256,768]{1,0:T(8,128)(2,1)S(1)} %get-tuple-element.63), channel_id=1, source_target_pairs={{0,80},{16,64},{32,112},{48,96},{64,16},{80,0},{96,48},{112,32},{1... | collective-permute-start | bytes 1179656 | tf_op jit(solution)/shard_map/ppermute | solution.py:295
  33.5 3.7 %collective-permute-done.5.refs_2_ = bf16[256,768]{1,0:T(8,128)(2,1)S(1)} collective-permute-done((bf16[256,768]{1,0:T(8,128)(2,1)S(1)}, bf16[256,768]{1,0:T(8,128)(2,1)S(1)}, u32[]{:S(2)}, u32[]{:S(2)}) %collective-permute-start.5) | collective-permute-done | bytes 393248 | tf_op jit(solution)/shard_map/ppermute | solution.py:295
  37.1 1.2 collective-permute-start.11
  38.3 0.0 collective-permute-done.6.refs_3_
  38.3 0.9 collective-permute-start.12
  39.3 0.0 collective-permute-done.7.refs_4_
  39.3 2.0 %collective-permute-start.13 = (bf16[256,768]{1,0:T(8,128)(2,1)S(1)}, bf16[256,768]{1,0:T(8,128)(2,1)S(1)}, u32[]{:S(2)}, u32[]{:S(2)}) collective-permute-start(bf16[256,768]{1,0:T(8,128)(2,1)S(1)} %get-tuple-element.77), channel_id=1, source_target_pairs={{0,112},{16,96},{32,16},{48,0},{64,48},{80,32},{96,80},{112,64},{1... | collective-permute-start | bytes 1179656 | tf_op jit(solution)/shard_map/ppermute | solution.py:295
  41.3 0.0 copy-done
  41.3 0.7 norms.1
  42.0 0.8 copy-done.3
  42.8 4.0 %stats_0.2 = (f32[1024,768]{1,0:T(8,128)S(1)}, f32[1024,128]{1,0:T(8,128)S(1)}) custom-call(bf16[2,1024,768]{2,1,0:T(8,128)(2,1)S(1)} %copy-done, f32[1024,128]{1,0:T(8,128)S(1)} %get-tuple-element.61.refs_1_, bf16[256,768]{1,0:T(8,128)(2,1)S(1)} %get-tuple-element.67.refs_2_, bf16[256,768]{1,0:T(8,128)(2,1)S(1)} %collective-permute-done.8.refs_3_, ...), custom_call_target="tpu_custom_call" | custom-call | tf_op jit(solution)/shard_map/stats_0/pallas_call | solution.py:194
  46.7 4.0 %stats_0.3 = (f32[1024,768]{1,0:T(8,128)S(1)}, f32[1024,128]{1,0:T(8,128)S(1)}) custom-call(bf16[2,1024,768]{2,1,0:T(8,128)(2,1)S(1)} %copy-done, f32[1024,128]{1,0:T(8,128)S(1)} %get-tuple-element.61.refs_1_, bf16[256,768]{1,0:T(8,128)(2,1)S(1)} %collective-permute-done.5.refs_2_, bf16[256,768]{1,0:T(8,128)(2,1)S(1)} %collective-permute-done.6.refs_3_, ...), custom_call_target="tpu_custom_call" | custom-call | tf_op jit(solution)/shard_map/stats_0/pallas_call | solution.py:194
  50.7 3.9 %collective-permute-done.4.refs_3_ = bf16[256,768]{1,0:T(8,128)(2,1)S(1)} collective-permute-done((bf16[256,768]{1,0:T(8,128)(2,1)S(1)}, bf16[256,768]{1,0:T(8,128)(2,1)S(1)}, u32[]{:S(2)}, u32[]{:S(2)}) %collective-permute-start.4) | collective-permute-done | bytes 393248 | tf_op jit(solution)/shard_map/ppermute | solution.py:295
  54.7 4.6 %last_0.1 = bf16[16,400,128]{2,1,0:T(8,128)(2,1)S(1)} custom-call(bf16[2,1024,768]{2,1,0:T(8,128)(2,1)S(1)} %copy-done, f32[1024,128]{1,0:T(8,128)S(1)} %get-tuple-element.61.refs_1_, bf16[256,768]{1,0:T(8,128)(2,1)S(1)} %collective-permute-done.3.refs_2_, bf16[256,768]{1,0:T(8,128)(2,1)S(1)} %collective-permute-done.4.refs_3_, ...), custom_call_target="tpu_custom_call" | custom-call | tf_op jit(solution)/shard_map/last_0/pallas_call | solution.py:210
  59.3 1.2 copy-done.1
  60.5 0.0 collective-permute-done.10.refs_3_
  60.5 0.8 copy-done.6
  61.2 0.0 collective-permute-done.11.refs_4_
  61.2 0.7 copy-done.8
  62.0 0.3 collective-permute-done.12.refs_5_
  62.3 0.7 copy-done.10
  63.0 0.0 collective-permute-done.13.refs_6_
  63.0 0.8 copy-done.12
  63.8 7.6 %all-to-all-start.1 = ((bf16[16,400,128]{2,1,0:T(8,128)(2,1)}), bf16[16,400,128]{2,1,0:T(8,128)(2,1)}, u32[]{:S(2)}, u32[]{:S(2)}) async-start(bf16[16,400,128]{2,1,0:T(8,128)(2,1)} %copy-done.1), calls=%async_computation.1 | async-start | bytes 3276800 | tf_op jit(solution)/shard_map/all_to_all | solution.py:330
  71.4 1.4 %collective-permute-start = (bf16[256,768]{1,0:T(8,128)(2,1)}, bf16[256,768]{1,0:T(8,128)(2,1)S(1)}, u32[]{:S(2)}, u32[]{:S(2)}) collective-permute-start(bf16[256,768]{1,0:T(8,128)(2,1)} %copy-done.18), channel_id=1, source_target_pairs={{0,64},{16,80},{32,96},{48,112},{64,0},{80,16},{96,32},{112,48},{1... | collective-permute-start | bytes 1179656 | tf_op jit(solution)/shard_map/ppermute | solution.py:295
  72.8 3.7 %collective-permute-start.1 = (bf16[256,768]{1,0:T(8,128)(2,1)}, bf16[256,768]{1,0:T(8,128)(2,1)S(1)}, u32[]{:S(2)}, u32[]{:S(2)}) collective-permute-start(bf16[256,768]{1,0:T(8,128)(2,1)} %copy-done.17), channel_id=1, source_target_pairs={{0,80},{16,64},{32,112},{48,96},{64,16},{80,0},{96,48},{112,32},{1... | collective-permute-start | bytes 1179656 | tf_op jit(solution)/shard_map/ppermute | solution.py:295
  76.6 0.0 collective-permute-start.2
  76.6 1.0 copy-done.4
  77.6 1.0 copy-done.7
  78.6 1.0 copy-done.9
  79.6 1.0 copy-done.11
  80.6 1.0 copy-done.13
  81.6 5.5 %stats_1.1 = (f32[1024,768]{1,0:T(8,128)S(1)}, f32[1024,128]{1,0:T(8,128)S(1)}) custom-call(bf16[2,1024,768]{2,1,0:T(8,128)(2,1)S(1)} %copy-done, f32[1024,128]{1,0:T(8,128)S(1)} %copy-done.4, bf16[256,768]{1,0:T(8,128)(2,1)S(1)} %get-tuple-element.60.refs_2_, bf16[256,768]{1,0:T(8,128)(2,1)S(1)} %copy-done.7, bf16[256,768]{1,0:T(8,128)(2,1)S(1)} %copy-done.9, ...), custom_call_target="tpu_custom_call" | custom-call | tf_op jit(solution)/shard_map/stats_1/pallas_call | solution.py:194
  87.1 0.0 collective-permute-done.refs_2_
  87.1 5.7 %collective-permute-done.1.refs_3_ = bf16[256,768]{1,0:T(8,128)(2,1)S(1)} collective-permute-done((bf16[256,768]{1,0:T(8,128)(2,1)}, bf16[256,768]{1,0:T(8,128)(2,1)S(1)}, u32[]{:S(2)}, u32[]{:S(2)}) %collective-permute-start.1) | collective-permute-done | bytes 393248 | tf_op jit(solution)/shard_map/ppermute | solution.py:295
  92.9 0.0 collective-permute-done.2.refs_4_
  92.9 6.0 %last_1.1 = bf16[16,400,128]{2,1,0:T(8,128)(2,1)S(1)} custom-call(bf16[2,1024,768]{2,1,0:T(8,128)(2,1)S(1)} %copy-done, f32[1024,128]{1,0:T(8,128)S(1)} %copy-done.5, bf16[256,768]{1,0:T(8,128)(2,1)S(1)} %collective-permute-done.refs_2_, bf16[256,768]{1,0:T(8,128)(2,1)S(1)} %collective-permute-done.1.refs_3_, ...), custom_call_target="tpu_custom_call" | custom-call | tf_op jit(solution)/shard_map/last_1/pallas_call | solution.py:210
  98.9 1.2 copy-done.2
  100.1 0.0 all-to-all-done.1.got_ref
  100.1 6.2 %all-to-all-start = ((bf16[16,400,128]{2,1,0:T(8,128)(2,1)}), bf16[16,400,128]{2,1,0:T(8,128)(2,1)}, u32[]{:S(2)}, u32[]{:S(2)}) async-start(bf16[16,400,128]{2,1,0:T(8,128)(2,1)} %copy-done.2), calls=%async_computation | async-start | bytes 3276800 | tf_op jit(solution)/shard_map/all_to_all | solution.py:330
  106.3 2.2 %finish_0.1.rest_0_ = f32[2,64,768]{2,1,0:T(8,128)} custom-call(s32[1]{0:T(128)} %bitcast.me_ref, bf16[16,400,128]{2,1,0:T(8,128)(2,1)} %all-to-all-done.1.got_ref, bf16[2,1024,768]{2,1,0:T(8,128)(2,1)S(1)} %copy-done), custom_call_target="tpu_custom_call" | custom-call | tf_op jit(solution)/shard_map/finish_0/pallas_call | solution.py:268
  108.5 22.5 %all-to-all-done.got_ref = bf16[16,400,128]{2,1,0:T(8,128)(2,1)} async-done(((bf16[16,400,128]{2,1,0:T(8,128)(2,1)}), bf16[16,400,128]{2,1,0:T(8,128)(2,1)}, u32[]{:S(2)}, u32[]{:S(2)}) %all-to-all-start) | async-done | bytes 1638432 | tf_op jit(solution)/shard_map/all_to_all | solution.py:330
  131.1 2.2 %finish_1.1 = f32[2,64,768]{2,1,0:T(8,128)} custom-call(s32[1]{0:T(128)} %bitcast.me_ref, bf16[16,400,128]{2,1,0:T(8,128)(2,1)} %all-to-all-done.got_ref, bf16[2,1024,768]{2,1,0:T(8,128)(2,1)S(1)} %copy-done, f32[2,64,768]{2,1,0:T(8,128)} %finish_0.1.rest_0_), custom_call_target="tpu_custom_call", output_to_operand_aliasing={{}: (3, {})} | custom-call | tf_op jit(solution)/shard_map/finish_1/pallas_call | solution.py:268
  (21 shorter events, 0.0 us)
Async XLA Ops:
  0.7 1.9 %copy-start.14 = (bf16[2048,768]{1,0:T(8,128)(2,1)S(1)}, bf16[2048,768]{1,0:T(8,128)(2,1)}, u32[]{:S(2)}) copy-start(bf16[2048,768]{1,0:T(8,128)(2,1)} %refs_1_.5) | copy-start | bytes 9437188
  2.6 0.7 copy-start.19
  5.8 13.9 %collective-permute-start.8 = (bf16[256,768]{1,0:T(8,128)(2,1)S(1)}, bf16[256,768]{1,0:T(8,128)(2,1)S(1)}, u32[]{:S(2)}, u32[]{:S(2)}) collective-permute-start(bf16[256,768]{1,0:T(8,128)(2,1)S(1)} %get-tuple-element.68), channel_id=1, source_target_pairs={{0,32},{16,48},{32,64},{48,80},{64,96},{80,112},{96,0},{112,16},{1... | collective-permute-start | bytes 1179656 | tf_op jit(solution)/shard_map/ppermute | solution.py:295
  8.0 23.4 %collective-permute-start.9 = (bf16[256,768]{1,0:T(8,128)(2,1)S(1)}, bf16[256,768]{1,0:T(8,128)(2,1)S(1)}, u32[]{:S(2)}, u32[]{:S(2)}) collective-permute-start(bf16[256,768]{1,0:T(8,128)(2,1)S(1)} %get-tuple-element.69), channel_id=1, source_target_pairs={{0,96},{16,112},{32,0},{48,16},{64,32},{80,48},{96,64},{112,80},{1... | collective-permute-start | bytes 1179656 | tf_op jit(solution)/shard_map/ppermute | solution.py:295
  15.1 16.4 %collective-permute-start.3 = (bf16[256,768]{1,0:T(8,128)(2,1)S(1)}, bf16[256,768]{1,0:T(8,128)(2,1)S(1)}, u32[]{:S(2)}, u32[]{:S(2)}) collective-permute-start(bf16[256,768]{1,0:T(8,128)(2,1)S(1)} %get-tuple-element.62), channel_id=1, source_target_pairs={{0,64},{16,80},{32,96},{48,112},{64,0},{80,16},{96,32},{112,48},{1... | collective-permute-start | bytes 1179656 | tf_op jit(solution)/shard_map/ppermute | solution.py:295
  16.8 20.3 %collective-permute-start.5 = (bf16[256,768]{1,0:T(8,128)(2,1)S(1)}, bf16[256,768]{1,0:T(8,128)(2,1)S(1)}, u32[]{:S(2)}, u32[]{:S(2)}) collective-permute-start(bf16[256,768]{1,0:T(8,128)(2,1)S(1)} %get-tuple-element.64), channel_id=1, source_target_pairs={{0,48},{16,32},{32,80},{48,64},{64,112},{80,96},{96,16},{112,0},{1... | collective-permute-start | bytes 1179656 | tf_op jit(solution)/shard_map/ppermute | solution.py:295
  18.6 19.8 %collective-permute-start.6 = (bf16[256,768]{1,0:T(8,128)(2,1)S(1)}, bf16[256,768]{1,0:T(8,128)(2,1)S(1)}, u32[]{:S(2)}, u32[]{:S(2)}) collective-permute-start(bf16[256,768]{1,0:T(8,128)(2,1)S(1)} %get-tuple-element.65), channel_id=1, source_target_pairs={{0,112},{16,96},{32,16},{48,0},{64,48},{80,32},{96,80},{112,64},{1... | collective-permute-start | bytes 1179656 | tf_op jit(solution)/shard_map/ppermute | solution.py:295
  19.8 7.7 %copy-start.15 = (bf16[2048,768]{1,0:T(8,128)(2,1)S(1)}, bf16[2048,768]{1,0:T(8,128)(2,1)}, u32[]{:S(2)}) copy-start(bf16[2048,768]{1,0:T(8,128)(2,1)} %refs_1_.5) | copy-start | bytes 9437188
  19.8 19.5 %collective-permute-start.7 = (bf16[256,768]{1,0:T(8,128)(2,1)S(1)}, bf16[256,768]{1,0:T(8,128)(2,1)S(1)}, u32[]{:S(2)}, u32[]{:S(2)}) collective-permute-start(bf16[256,768]{1,0:T(8,128)(2,1)S(1)} %get-tuple-element.66), channel_id=1, source_target_pairs={{0,16},{16,0},{32,48},{48,32},{64,80},{80,64},{96,112},{112,96},{1... | collective-permute-start | bytes 1179656 | tf_op jit(solution)/shard_map/ppermute | solution.py:295
  25.2 0.7 copy-start.16
  26.0 0.8 copy-start.17
  26.7 0.7 copy-start.18
  27.5 13.8 %copy-start = (bf16[2,1024,768]{2,1,0:T(8,128)(2,1)S(1)}, bf16[2,1024,768]{2,1,0:T(8,128)(2,1)}, u32[]{:S(2)}) copy-start(bf16[2,1024,768]{2,1,0:T(8,128)(2,1)} %cents_ref.5) | copy-start | bytes 9437188
  31.4 29.0 %collective-permute-start.10 = (bf16[256,768]{1,0:T(8,128)(2,1)S(1)}, bf16[256,768]{1,0:T(8,128)(2,1)S(1)}, u32[]{:S(2)}, u32[]{:S(2)}) collective-permute-start(bf16[256,768]{1,0:T(8,128)(2,1)S(1)} %get-tuple-element.74), channel_id=1, source_target_pairs={{0,32},{16,48},{32,64},{48,80},{64,96},{80,112},{96,0},{112,16},{1... | collective-permute-start | bytes 1179656 | tf_op jit(solution)/shard_map/ppermute | solution.py:295
  31.5 23.1 %collective-permute-start.4 = (bf16[256,768]{1,0:T(8,128)(2,1)S(1)}, bf16[256,768]{1,0:T(8,128)(2,1)S(1)}, u32[]{:S(2)}, u32[]{:S(2)}) collective-permute-start(bf16[256,768]{1,0:T(8,128)(2,1)S(1)} %get-tuple-element.63), channel_id=1, source_target_pairs={{0,80},{16,64},{32,112},{48,96},{64,16},{80,0},{96,48},{112,32},{1... | collective-permute-start | bytes 1179656 | tf_op jit(solution)/shard_map/ppermute | solution.py:295
  37.1 24.1 %collective-permute-start.11 = (bf16[256,768]{1,0:T(8,128)(2,1)S(1)}, bf16[256,768]{1,0:T(8,128)(2,1)S(1)}, u32[]{:S(2)}, u32[]{:S(2)}) collective-permute-start(bf16[256,768]{1,0:T(8,128)(2,1)S(1)} %get-tuple-element.75), channel_id=1, source_target_pairs={{0,96},{16,112},{32,0},{48,16},{64,32},{80,48},{96,64},{112,80},{1... | collective-permute-start | bytes 1179656 | tf_op jit(solution)/shard_map/ppermute | solution.py:295
  38.3 23.9 %collective-permute-start.12 = (bf16[256,768]{1,0:T(8,128)(2,1)S(1)}, bf16[256,768]{1,0:T(8,128)(2,1)S(1)}, u32[]{:S(2)}, u32[]{:S(2)}) collective-permute-start(bf16[256,768]{1,0:T(8,128)(2,1)S(1)} %get-tuple-element.76), channel_id=1, source_target_pairs={{0,48},{16,32},{32,80},{48,64},{64,112},{80,96},{96,16},{112,0},{1... | collective-permute-start | bytes 1179656 | tf_op jit(solution)/shard_map/ppermute | solution.py:295
  39.3 23.7 %collective-permute-start.13 = (bf16[256,768]{1,0:T(8,128)(2,1)S(1)}, bf16[256,768]{1,0:T(8,128)(2,1)S(1)}, u32[]{:S(2)}, u32[]{:S(2)}) collective-permute-start(bf16[256,768]{1,0:T(8,128)(2,1)S(1)} %get-tuple-element.77), channel_id=1, source_target_pairs={{0,112},{16,96},{32,16},{48,0},{64,48},{80,32},{96,80},{112,64},{1... | collective-permute-start | bytes 1179656 | tf_op jit(solution)/shard_map/ppermute | solution.py:295
  42.0 0.8 copy-start.3
  59.3 1.2 copy-start.1
  60.5 0.8 copy-start.6
  61.2 0.8 copy-start.8
  62.3 0.7 copy-start.10
  63.0 0.8 copy-start.12
  63.8 36.4 %all-to-all-start.1 = ((bf16[16,400,128]{2,1,0:T(8,128)(2,1)}), bf16[16,400,128]{2,1,0:T(8,128)(2,1)}, u32[]{:S(2)}, u32[]{:S(2)}) async-start(bf16[16,400,128]{2,1,0:T(8,128)(2,1)} %copy-done.1), calls=%async_computation.1 | async-start | bytes 3276800 | tf_op jit(solution)/shard_map/all_to_all | solution.py:330
  71.4 15.7 %collective-permute-start = (bf16[256,768]{1,0:T(8,128)(2,1)}, bf16[256,768]{1,0:T(8,128)(2,1)S(1)}, u32[]{:S(2)}, u32[]{:S(2)}) collective-permute-start(bf16[256,768]{1,0:T(8,128)(2,1)} %copy-done.18), channel_id=1, source_target_pairs={{0,64},{16,80},{32,96},{48,112},{64,0},{80,16},{96,32},{112,48},{1... | collective-permute-start | bytes 1179656 | tf_op jit(solution)/shard_map/ppermute | solution.py:295
  72.8 20.1 %collective-permute-start.1 = (bf16[256,768]{1,0:T(8,128)(2,1)}, bf16[256,768]{1,0:T(8,128)(2,1)S(1)}, u32[]{:S(2)}, u32[]{:S(2)}) collective-permute-start(bf16[256,768]{1,0:T(8,128)(2,1)} %copy-done.17), channel_id=1, source_target_pairs={{0,80},{16,64},{32,112},{48,96},{64,16},{80,0},{96,48},{112,32},{1... | collective-permute-start | bytes 1179656 | tf_op jit(solution)/shard_map/ppermute | solution.py:295
  76.6 16.3 %collective-permute-start.2 = (bf16[256,768]{1,0:T(8,128)(2,1)}, bf16[256,768]{1,0:T(8,128)(2,1)S(1)}, u32[]{:S(2)}, u32[]{:S(2)}) collective-permute-start(bf16[256,768]{1,0:T(8,128)(2,1)} %copy-done.16), channel_id=1, source_target_pairs={{0,16},{16,0},{32,48},{48,32},{64,80},{80,64},{96,112},{112,96},{1... | collective-permute-start | bytes 1179656 | tf_op jit(solution)/shard_map/ppermute | solution.py:295
  76.6 1.0 copy-start.4
  77.6 1.0 copy-start.7
  78.6 1.0 copy-start.9
  79.6 1.0 copy-start.11
  80.6 1.0 copy-start.13
  81.6 11.3 %copy-start.5 = (f32[1024,128]{1,0:T(8,128)S(1)}, f32[1024,128]{1,0:T(8,128)}, u32[]{:S(2)}) copy-start(f32[1024,128]{1,0:T(8,128)} %copy-done.3) | copy-start | bytes 1572868
  98.9 1.2 copy-start.2
  100.1 30.9 %all-to-all-start = ((bf16[16,400,128]{2,1,0:T(8,128)(2,1)}), bf16[16,400,128]{2,1,0:T(8,128)(2,1)}, u32[]{:S(2)}, u32[]{:S(2)}) async-start(bf16[16,400,128]{2,1,0:T(8,128)(2,1)} %copy-done.2), calls=%async_computation | async-start | bytes 3276800 | tf_op jit(solution)/shard_map/all_to_all | solution.py:330
where the time goes:
time: 134 us; the launch traced here: 133 us
  Pallas kernels  45.2 us (34%)
  waiting for transfers between devices  36.2 us (27%)
  starting transfers between devices  35 us (26%)
  local copies, waits for them, and re-layouts  16.8 us (13%)
    all_to_all x2, waiting for transfers between devices, per_device(): lax.all_to_all(part, 'shard', split_axis=0, concat_axis=0, tiled=True)  22.5 us
    ppermute x14, starting transfers between devices, hop(): lax.ppermute(block, 'list', [(g, target(g, step, groups)) for g in range(...  21.2 us
    unnamed x40, local copies, waits for them, and re-layouts  16.1 us
    pallas_call x4, Pallas kernels, pack(): pl.pallas_call(functools.partial(pack_kernel, keys is None, at), out_shap...  16 us
    all_to_all x2, starting transfers between devices, per_device(): lax.all_to_all(part, 'shard', split_axis=0, concat_axis=0, tiled=True)  13.8 us
    ppermute x14, waiting for transfers between devices, hop(): lax.ppermute(block, 'list', [(g, target(g, step, groups)) for g in range(...  13.6 us
    pallas_call x3, Pallas kernels, stats(): pl.pallas_call(functools.partial(stats_kernel, index, len(rows), carried...  13.5 us
    pallas_call x2, Pallas kernels, last_stats(): pl.pallas_call(functools.partial(last_kernel, index, len(rows), shares),...  10.6 us
  transfers between devices with their start and end apart: 16, of which 5 were waited for; matrix products, arithmetic and copies ran while one was open for 0% of the time, Pallas kernels for 30%

commit v1 on v0

--- a/solution.py
+++ b/solution.py
@@ -3,7 +3,6 @@
 
 import jax
 import jax.numpy as jnp
-import numpy as np
 from jax import lax
 from jax.experimental import pallas as pl
 from jax.experimental.pallas import tpu as pltpu
@@ -18,7 +17,7 @@
 TAIL_ROWS = 16
 PIECES = 4
 HOPS = ((1, 0), (3, 0), (1, 1), (3, 1), (2, 0), (2, 1), (0, 1), (0, 0))
-STAGES = (((7, 0, 1), (2, 3, 6), (4, 5)), ((7, 0, 1, 2, 3), (4, 5, 6)))
+STAGES = (((7, 0, 1), (2, 3, 6), (4, 5)), ((7, 0, 1, 2, 3, 6), (4, 5)))
 TIED = 4
 FIRST = 2
 VMEM = pl.BlockSpec(memory_space=pltpu.VMEM)
@@ -41,18 +40,26 @@
     count_ref[...] = jnp.broadcast_to(seen, count_ref.shape).astype(jnp.int32)
 
 
-def pack_kernel(first, at, *refs):
+def pack_kernel(first, hops, index, local, *refs):
     if first:
-        names_ref, ids_ref, rows_ref, key_ref, count_ref, *outs = refs
+        ids_ref, rows_hbm, key_ref, count_ref, *outs, rows_ref, sem = refs
+        load = pltpu.make_async_copy(rows_hbm, rows_ref, sem)
+        load.start()
         count_into(key_ref, count_ref, ids_ref)
     else:
-        names_ref, rows_ref, key_ref, count_ref, *outs = refs
+        rows_ref, key_ref, count_ref, *outs = refs
+    lists = key_ref.shape[0]
     cap = outs[0].shape[0]
+    me = lax.axis_index("list")
+    y, core = lax.div(me, 2), lax.rem(me, 2)
     slots = lax.broadcasted_iota(jnp.int32, (cap, rows_ref.shape[0]), 0)
     lane = lax.broadcasted_iota(jnp.int32, (cap, LANES), 1)
     slot = lax.broadcasted_iota(jnp.int32, (cap, LANES), 0)
-    for k, out_ref in enumerate(outs):
-        name = names_ref[at + k]
+    if first:
+        load.wait()
+    for (dy, dc), out_ref in zip(hops, outs):
+        to_core = 1 - core if dc else core
+        name = (lax.rem(y + dy, lists // local // 2) * 2 + to_core) * local + index
         pick = jnp.where(key_ref[pl.ds(name, 1), :] == slots, 1.0, 0.0).astype(jnp.bfloat16)
         out = jnp.dot(pick, rows_ref[...], preferred_element_type=jnp.float32)
         out_ref[...] = out.astype(jnp.bfloat16)
@@ -60,17 +67,20 @@
         out_ref[:, :LANES] = jnp.where(padding, PAD_MARK, out[:, :LANES]).astype(jnp.bfloat16)
 
 
-def pack(names, at, blocks, rows, lists, cap, ids=None, keys=None):
+def pack(hops, index, local, rows, lists, cap, ids=None, keys=None):
     count, width = rows.shape
+    blocks = len(hops)
     made = [jax.ShapeDtypeStruct((cap, width), jnp.bfloat16)] * blocks
     kept = [jax.ShapeDtypeStruct((lists, count), jnp.int32), jax.ShapeDtypeStruct((lists, LANES), jnp.int32)]
-    operands = [names] + ([ids, rows] if keys is None else [rows, *keys])
-    made = (kept if keys is None else []) + made
+    first = keys is None
+    operands = [ids, rows] if first else [rows, *keys]
+    made = (kept if first else []) + made
     out = pl.pallas_call(
-        functools.partial(pack_kernel, keys is None, at),
+        functools.partial(pack_kernel, first, hops, index, local),
         out_shape=made,
-        in_specs=[SMEM] + [VMEM] * (len(operands) - 1),
+        in_specs=[VMEM, pl.BlockSpec(memory_space=pl.ANY)] if first else [VMEM] * len(operands),
         out_specs=[VMEM] * len(made),
+        scratch_shapes=[pltpu.VMEM((count, width), jnp.bfloat16), pltpu.SemaphoreType.DMA] if first else [],
         compiler_params=PARAMS,
         cost_estimate=pl.CostEstimate(
             flops=2 * blocks * cap * count * width, bytes_accessed=2 * rows.size, transcendentals=0
@@ -78,7 +88,7 @@
         name="pack",
     )(*operands)
     out = list(out)
-    return (out[:2], out[2:]) if keys is None else out
+    return (out[:2], out[2:]) if first else out
 
 
 def norm_kernel(cents_ref, *outs):
@@ -209,7 +219,7 @@
     operands = [cents, norm, *rows, *carried]
     return pl.pallas_call(
         functools.partial(last_kernel, index, len(rows), shares),
-        out_shape=jax.ShapeDtypeStruct(sent, jnp.bfloat16),
+        out_shape=pltpu.HBM(sent, jnp.bfloat16),
         in_specs=[VMEM] * (2 + len(rows)) + [pl.BlockSpec(memory_space=pl.ANY), VMEM],
         out_specs=pl.BlockSpec(memory_space=pltpu.HBM),
         scratch_shapes=[
@@ -302,17 +312,13 @@
     lists = local * groups
     cap = embeddings.shape[0] // 8
     ids = list_ids.reshape(1, -1)
-    g = lax.axis_index("list").astype(jnp.int32)
     me = lax.axis_index("shard").astype(jnp.int32).reshape(1)
-    table = [[target(k, step, groups) for step in HOPS] for k in range(groups)]
-    table = np.array([[d * local + i for i in range(local) for d in row] for row in table], np.int32)
-    names = lax.dynamic_index_in_dim(jnp.asarray(table), g, 0, keepdims=False)
     tie = lax.optimization_barrier
-    keys, sent = pack(names, 0, FIRST, embeddings, lists, cap, ids=ids)
-    sent = sent + pack(names, FIRST, groups - FIRST, embeddings, lists, cap, keys=keys)
+    keys, sent = pack(HOPS[:FIRST], 0, local, embeddings, lists, cap, ids=ids)
+    sent += pack(HOPS[FIRST:], 0, local, embeddings, lists, cap, keys=keys)
     later = []
     for at in range(0, groups, TIED):
-        later += pack(names, groups + at, TIED, embeddings, lists, cap, keys=keys)
+        later += pack(HOPS[at : at + TIED], 1, local, embeddings, lists, cap, keys=keys)
     sent[-1], later = tie((sent[-1], later))
     norm = norms(centroids)
     rows = [[hop(b, step, groups) for b, step in zip(blocks, HOPS)] for blocks in (sent, later)]

time: 134 us -> 130 us (0.970)
  starting transfers between devices: 35 us -> 43.7 us
  local copies, waits for them, and re-layouts: 16.8 us -> 11.5 us
  Pallas kernels: 45.2 us -> 40.3 us
  waiting for transfers between devices: 36.2 us -> 32.8 us
    ppermute x14, starting transfers between devices: 21.2 us -> 29.6 us  [hop(): lax.ppermute(block, 'list', [(g, target(g, step, groups)) for g in range(...]
    unnamed x40 -> x34, local copies, waits for them, and re-layouts: 16.1 us -> 11.5 us
    pallas_call x2, Pallas kernels: 10.6 us -> 7.47 us  [last_stats(): pl.pallas_call(functools.partial(last_kernel, index, len(rows), shares),...]
    ppermute x14, waiting for transfers between devices: 13.6 us -> 11 us  [hop(): lax.ppermute(block, 'list', [(g, target(g, step, groups)) for g in range(...]
    pallas_call x4, Pallas kernels: 16 us -> 14.1 us  [pack(): pl.pallas_call(functools.partial(pack_kernel, first, hops, index, local),...]
  transfers between devices with their start and end apart: 16 -> 16, of which waited for: 5 -> 5; matrix products, arithmetic and copies ran while one was open for 0% -> 0% of each run, Pallas kernels for 30% -> 28%
where the time goes in v1:
time: 130 us; the launch traced here: 129 us
  starting transfers between devices  43.7 us (34%)
  Pallas kernels  40.3 us (31%)
  waiting for transfers between devices  32.8 us (25%)
  local copies, waits for them, and re-layouts  11.5 us (9%)
    ppermute x14, starting transfers between devices, hop(): lax.ppermute(block, 'list', [(g, target(g, step, groups)) for g in range(...  29.6 us
    all_to_all x2, waiting for transfers between devices, per_device(): lax.all_to_all(part, 'shard', split_axis=0, concat_axis=0, tiled=True)  21.8 us
    pallas_call x4, Pallas kernels, pack(): pl.pallas_call(functools.partial(pack_kernel, first, hops, index, local),...  14.1 us
    all_to_all x2, starting transfers between devices, per_device(): lax.all_to_all(part, 'shard', split_axis=0, concat_axis=0, tiled=True)  14.1 us
    pallas_call x3, Pallas kernels, stats(): pl.pallas_call(functools.partial(stats_kernel, index, len(rows), carried...  13.6 us
    unnamed x34, local copies, waits for them, and re-layouts  11.5 us
    ppermute x14, waiting for transfers between devices, hop(): lax.ppermute(block, 'list', [(g, target(g, step, groups)) for g in range(...  11 us
    pallas_call x2, Pallas kernels, last_stats(): pl.pallas_call(functools.partial(last_kernel, index, len(rows), shares),...  7.47 us
  transfers between devices with their start and end apart: 16, of which 5 were waited for; matrix products, arithmetic and copies ran while one was open for 0% of the time, Pallas kernels for 28%

profile of v1, /device:TPU:1, one launch (start us, length us, event | category | flops | bytes accessed | tf_op | source)
XLA Modules:
  0.0 128.7 jit_solution(12825629143766448448)
XLA Ops:
  0.0 1.9 %copy-done.11 = bf16[2048,768]{1,0:T(8,128)(2,1)S(1)} copy-done((bf16[2048,768]{1,0:T(8,128)(2,1)S(1)}, bf16[2048,768]{1,0:T(8,128)(2,1)}, u32[]{:S(2)}) %copy-start.11) | copy-done | bytes 3145752
  1.9 0.7 copy-done.16
  2.6 2.3 %pack.4 = (s32[16,2048]{1,0:T(8,128)S(1)}, s32[16,128]{1,0:T(8,128)S(1)}, bf16[256,768]{1,0:T(8,128)(2,1)S(1)}, bf16[256,768]{1,0:T(8,128)(2,1)S(1)}) custom-call(s32[1,2048]{1,0:T(1,128)S(1)} %bitcast.2, bf16[2048,768]{1,0:T(8,128)(2,1)S(1)} %copy-done.11), custom_call_target="tpu_custom_call" | custom-call | flops 1610612736 | bytes 3145728 | tf_op jit(solution)/shard_map/pack/pallas_call | solution.py:78
  4.9 2.2 %collective-permute-start.7 = (bf16[256,768]{1,0:T(8,128)(2,1)S(1)}, bf16[256,768]{1,0:T(8,128)(2,1)S(1)}, u32[]{:S(2)}, u32[]{:S(2)}) collective-permute-start(bf16[256,768]{1,0:T(8,128)(2,1)S(1)} %get-tuple-element.67), channel_id=1, source_target_pairs={{0,32},{16,48},{32,64},{48,80},{64,96},{80,112},{96,0},{112,16},{1... | collective-permute-start | bytes 1179656 | tf_op jit(solution)/shard_map/ppermute | solution.py:305
  7.1 1.5 %collective-permute-start.8 = (bf16[256,768]{1,0:T(8,128)(2,1)S(1)}, bf16[256,768]{1,0:T(8,128)(2,1)S(1)}, u32[]{:S(2)}, u32[]{:S(2)}) collective-permute-start(bf16[256,768]{1,0:T(8,128)(2,1)S(1)} %get-tuple-element.68), channel_id=1, source_target_pairs={{0,96},{16,112},{32,0},{48,16},{64,32},{80,48},{96,64},{112,80},{1... | collective-permute-start | bytes 1179656 | tf_op jit(solution)/shard_map/ppermute | solution.py:305
  8.6 0.0 copy-done.12
  8.6 5.0 %pack.5 = (bf16[256,768]{1,0:T(8,128)(2,1)S(1)}, bf16[256,768]{1,0:T(8,128)(2,1)S(1)}, bf16[256,768]{1,0:T(8,128)(2,1)S(1)}, bf16[256,768]{1,0:T(8,128)(2,1)S(1)...) custom-call(bf16[2048,768]{1,0:T(8,128)(2,1)S(1)} %copy-done.12, s32[16,2048]{1,0:T(8,128)S(1)} %get-tuple-element.46.refs_1_, ...), custom_call_target="tpu_custom_call" | custom-call | flops 4831838208 | bytes 3145728 | tf_op jit(solution)/shard_map/pack/pallas_call | solution.py:78
  13.6 1.1 collective-permute-start.4
  14.8 1.9 %collective-permute-start.5 = (bf16[256,768]{1,0:T(8,128)(2,1)S(1)}, bf16[256,768]{1,0:T(8,128)(2,1)S(1)}, u32[]{:S(2)}, u32[]{:S(2)}) collective-permute-start(bf16[256,768]{1,0:T(8,128)(2,1)S(1)} %get-tuple-element.64), channel_id=1, source_target_pairs={{0,112},{16,96},{32,16},{48,0},{64,48},{80,32},{96,80},{112,64},{1... | collective-permute-start | bytes 1179656 | tf_op jit(solution)/shard_map/ppermute | solution.py:305
  16.7 1.0 collective-permute-start.6
  17.7 0.0 collective-permute-done.7.refs_3_
  17.7 1.0 collective-permute-start.2
  18.7 3.4 %pack.6 = (bf16[256,768]{1,0:T(8,128)(2,1)S(1)}, bf16[256,768]{1,0:T(8,128)(2,1)S(1)}, bf16[256,768]{1,0:T(8,128)(2,1)S(1)}, bf16[256,768]{1,0:T(8,128)(2,1)S(1)}) custom-call(bf16[2048,768]{1,0:T(8,128)(2,1)S(1)} %copy-done.12, s32[16,2048]{1,0:T(8,128)S(1)} %get-tuple-element.46.refs_1_, s32[16,128]{1,0:T(8,128)S(1)} %get-tuple-element.47.refs_2_), custom_call_target="tpu_custom_call" | custom-call | flops 3221225472 | bytes 3145728 | tf_op jit(solution)/shard_map/pack/pallas_call | solution.py:78
  22.1 0.0 copy-start
  22.1 3.4 %pack.7 = (bf16[256,768]{1,0:T(8,128)(2,1)S(1)}, bf16[256,768]{1,0:T(8,128)(2,1)S(1)}, bf16[256,768]{1,0:T(8,128)(2,1)S(1)}, bf16[256,768]{1,0:T(8,128)(2,1)S(1)}) custom-call(bf16[2048,768]{1,0:T(8,128)(2,1)S(1)} %copy-done.12, s32[16,2048]{1,0:T(8,128)S(1)} %get-tuple-element.46.refs_1_, s32[16,128]{1,0:T(8,128)S(1)} %get-tuple-element.47.refs_2_), custom_call_target="tpu_custom_call" | custom-call | flops 3221225472 | bytes 3145728 | tf_op jit(solution)/shard_map/pack/pallas_call | solution.py:78
  25.5 0.0 copy-start.13
  25.5 0.0 copy-start.14
  25.5 0.0 copy-start.15
  25.5 0.0 collective-permute-done.8.refs_4_
  25.6 3.1 %collective-permute-start.3 = (bf16[256,768]{1,0:T(8,128)(2,1)S(1)}, bf16[256,768]{1,0:T(8,128)(2,1)S(1)}, u32[]{:S(2)}, u32[]{:S(2)}) collective-permute-start(bf16[256,768]{1,0:T(8,128)(2,1)S(1)} %get-tuple-element.62), channel_id=1, source_target_pairs={{0,80},{16,64},{32,112},{48,96},{64,16},{80,0},{96,48},{112,32},{1... | collective-permute-start | bytes 1179656 | tf_op jit(solution)/shard_map/ppermute | solution.py:305
  28.7 0.0 collective-permute-done.4.refs_2_
  28.7 2.1 %collective-permute-start.10 = (bf16[256,768]{1,0:T(8,128)(2,1)S(1)}, bf16[256,768]{1,0:T(8,128)(2,1)S(1)}, u32[]{:S(2)}, u32[]{:S(2)}) collective-permute-start(bf16[256,768]{1,0:T(8,128)(2,1)S(1)} %get-tuple-element.74), channel_id=1, source_target_pairs={{0,96},{16,112},{32,0},{48,16},{64,32},{80,48},{96,64},{112,80},{1... | collective-permute-start | bytes 1179656 | tf_op jit(solution)/shard_map/ppermute | solution.py:305
  30.8 0.0 collective-permute-done.5.refs_3_
  30.8 0.0 collective-permute-start.11
  30.8 0.0 collective-permute-done.6.refs_4_
  30.8 3.0 %collective-permute-start.12 = (bf16[256,768]{1,0:T(8,128)(2,1)S(1)}, bf16[256,768]{1,0:T(8,128)(2,1)S(1)}, u32[]{:S(2)}, u32[]{:S(2)}) collective-permute-start(bf16[256,768]{1,0:T(8,128)(2,1)S(1)} %get-tuple-element.76), channel_id=1, source_target_pairs={{0,112},{16,96},{32,16},{48,0},{64,48},{80,32},{96,80},{112,64},{1... | collective-permute-start | bytes 1179656 | tf_op jit(solution)/shard_map/ppermute | solution.py:305
  33.8 1.8 %collective-permute-done.2.refs_2_ = bf16[256,768]{1,0:T(8,128)(2,1)S(1)} collective-permute-done((bf16[256,768]{1,0:T(8,128)(2,1)S(1)}, bf16[256,768]{1,0:T(8,128)(2,1)S(1)}, u32[]{:S(2)}, u32[]{:S(2)}) %collective-permute-start.2) | collective-permute-done | bytes 393248 | tf_op jit(solution)/shard_map/ppermute | solution.py:305
  35.5 8.4 %collective-permute-start.9 = (bf16[256,768]{1,0:T(8,128)(2,1)S(1)}, bf16[256,768]{1,0:T(8,128)(2,1)S(1)}, u32[]{:S(2)}, u32[]{:S(2)}) collective-permute-start(bf16[256,768]{1,0:T(8,128)(2,1)S(1)} %get-tuple-element.73), channel_id=1, source_target_pairs={{0,32},{16,48},{32,64},{48,80},{64,96},{80,112},{96,0},{112,16},{1... | collective-permute-start | bytes 1179656 | tf_op jit(solution)/shard_map/ppermute | solution.py:305
  44.0 0.0 copy-done
  44.0 0.7 norms.1
  44.6 0.8 copy-done.1
  45.4 4.0 %stats_0.2 = (f32[1024,768]{1,0:T(8,128)S(1)}, f32[1024,128]{1,0:T(8,128)S(1)}) custom-call(bf16[2,1024,768]{2,1,0:T(8,128)(2,1)S(1)} %copy-done, f32[1024,128]{1,0:T(8,128)S(1)} %get-tuple-element.60.refs_1_, bf16[256,768]{1,0:T(8,128)(2,1)S(1)} %get-tuple-element.66.refs_2_, bf16[256,768]{1,0:T(8,128)(2,1)S(1)} %collective-permute-done.7.refs_3_, ...), custom_call_target="tpu_custom_call" | custom-call | tf_op jit(solution)/shard_map/stats_0/pallas_call | solution.py:204
  49.4 0.0 copy-done.13
  49.4 0.0 copy-done.14
  49.4 4.0 %stats_0.3 = (f32[1024,768]{1,0:T(8,128)S(1)}, f32[1024,128]{1,0:T(8,128)S(1)}) custom-call(bf16[2,1024,768]{2,1,0:T(8,128)(2,1)S(1)} %copy-done, f32[1024,128]{1,0:T(8,128)S(1)} %get-tuple-element.60.refs_1_, bf16[256,768]{1,0:T(8,128)(2,1)S(1)} %collective-permute-done.4.refs_2_, bf16[256,768]{1,0:T(8,128)(2,1)S(1)} %collective-permute-done.5.refs_3_, ...), custom_call_target="tpu_custom_call" | custom-call | tf_op jit(solution)/shard_map/stats_0/pallas_call | solution.py:204
  53.4 0.0 collective-permute-done.3.refs_3_
  53.4 3.7 %last_0.1 = bf16[16,400,128]{2,1,0:T(8,128)(2,1)} custom-call(bf16[2,1024,768]{2,1,0:T(8,128)(2,1)S(1)} %copy-done, f32[1024,128]{1,0:T(8,128)S(1)} %get-tuple-element.60.refs_1_, bf16[256,768]{1,0:T(8,128)(2,1)S(1)} %collective-permute-done.2.refs_2_, bf16[256,768]{1,0:T(8,128)(2,1)S(1)} %collective-permute-done.3.refs_3_, ...), custom_call_target="tpu_custom_call" | custom-call | tf_op jit(solution)/shard_map/last_0/pallas_call | solution.py:220
  57.2 0.0 collective-permute-done.10.refs_4_
  57.2 0.7 copy-done.3
  57.9 0.0 collective-permute-done.11.refs_5_
  57.9 0.8 copy-done.5
  58.7 1.4 %collective-permute-done.12.refs_6_ = bf16[256,768]{1,0:T(8,128)(2,1)S(1)} collective-permute-done((bf16[256,768]{1,0:T(8,128)(2,1)S(1)}, bf16[256,768]{1,0:T(8,128)(2,1)S(1)}, u32[]{:S(2)}, u32[]{:S(2)}) %collective-permute-start.12) | collective-permute-done | bytes 393248 | tf_op jit(solution)/shard_map/ppermute | solution.py:305
  60.1 0.8 copy-done.7
  60.8 0.3 collective-permute-done.9.refs_3_
  61.2 0.8 copy-done.9
  61.9 7.6 %all-to-all-start.1 = ((bf16[16,400,128]{2,1,0:T(8,128)(2,1)}), bf16[16,400,128]{2,1,0:T(8,128)(2,1)}, u32[]{:S(2)}, u32[]{:S(2)}) async-start(bf16[16,400,128]{2,1,0:T(8,128)(2,1)} %last_0.1), calls=%async_computation.1 | async-start | bytes 3276800 | tf_op jit(solution)/shard_map/all_to_all | solution.py:336
  69.6 1.0 collective-permute-start.13
  70.6 2.3 %collective-permute-start = (bf16[256,768]{1,0:T(8,128)(2,1)}, bf16[256,768]{1,0:T(8,128)(2,1)S(1)}, u32[]{:S(2)}, u32[]{:S(2)}) collective-permute-start(bf16[256,768]{1,0:T(8,128)(2,1)} %copy-done.14), channel_id=1, source_target_pairs={{0,64},{16,80},{32,96},{48,112},{64,0},{80,16},{96,32},{112,48},{1... | collective-permute-start | bytes 1179656 | tf_op jit(solution)/shard_map/ppermute | solution.py:305
  72.9 0.9 collective-permute-start.1
  73.8 0.0 collective-permute-done.13.refs_7_
  73.8 1.0 copy-done.2
  74.9 1.0 copy-done.4
  75.9 1.0 copy-done.6
  76.9 1.0 copy-done.8
  77.9 1.0 copy-done.10
  78.9 5.7 %stats_1.1 = (f32[1024,768]{1,0:T(8,128)S(1)}, f32[1024,128]{1,0:T(8,128)S(1)}) custom-call(bf16[2,1024,768]{2,1,0:T(8,128)(2,1)S(1)} %copy-done, f32[1024,128]{1,0:T(8,128)S(1)} %copy-done.2, bf16[256,768]{1,0:T(8,128)(2,1)S(1)} %get-tuple-element.59.refs_2_, bf16[256,768]{1,0:T(8,128)(2,1)S(1)} %copy-done.10, bf16[256,768]{1,0:T(8,128)(2,1)S(1)} %copy-done.4, ...), custom_call_target="tpu_custom_call" | custom-call | tf_op jit(solution)/shard_map/stats_1/pallas_call | solution.py:204
  84.6 0.0 collective-permute-done.refs_2_
  84.6 7.4 %collective-permute-done.1.refs_3_ = bf16[256,768]{1,0:T(8,128)(2,1)S(1)} collective-permute-done((bf16[256,768]{1,0:T(8,128)(2,1)}, bf16[256,768]{1,0:T(8,128)(2,1)S(1)}, u32[]{:S(2)}, u32[]{:S(2)}) %collective-permute-start.1) | collective-permute-done | bytes 393248 | tf_op jit(solution)/shard_map/ppermute | solution.py:305
  92.0 3.7 %last_1.1 = bf16[16,400,128]{2,1,0:T(8,128)(2,1)} custom-call(bf16[2,1024,768]{2,1,0:T(8,128)(2,1)S(1)} %copy-done, f32[1024,128]{1,0:T(8,128)S(1)} %copy-done.2, bf16[256,768]{1,0:T(8,128)(2,1)S(1)} %collective-permute-done.refs_2_, bf16[256,768]{1,0:T(8,128)(2,1)S(1)} %collective-permute-done.1.refs_3_, f32[1024,768]{1,0:T(8,128)S(1)} %get-tuple-element.82.refs_4_, ...), custom_call_target="tpu_custom_call" | custom-call | tf_op jit(solution)/shard_map/last_1/pallas_call | solution.py:220
  95.7 0.0 all-to-all-done.1.got_ref
  95.8 6.5 %all-to-all-start = ((bf16[16,400,128]{2,1,0:T(8,128)(2,1)}), bf16[16,400,128]{2,1,0:T(8,128)(2,1)}, u32[]{:S(2)}, u32[]{:S(2)}) async-start(bf16[16,400,128]{2,1,0:T(8,128)(2,1)} %last_1.1), calls=%async_computation | async-start | bytes 3276800 | tf_op jit(solution)/shard_map/all_to_all | solution.py:336
  102.2 2.2 %finish_0.1.rest_0_ = f32[2,64,768]{2,1,0:T(8,128)} custom-call(s32[1]{0:T(128)} %bitcast.me_ref, bf16[16,400,128]{2,1,0:T(8,128)(2,1)} %all-to-all-done.1.got_ref, bf16[2,1024,768]{2,1,0:T(8,128)(2,1)S(1)} %copy-done), custom_call_target="tpu_custom_call" | custom-call | tf_op jit(solution)/shard_map/finish_0/pallas_call | solution.py:278
  104.4 21.8 %all-to-all-done.got_ref = bf16[16,400,128]{2,1,0:T(8,128)(2,1)} async-done(((bf16[16,400,128]{2,1,0:T(8,128)(2,1)}), bf16[16,400,128]{2,1,0:T(8,128)(2,1)}, u32[]{:S(2)}, u32[]{:S(2)}) %all-to-all-start) | async-done | bytes 1638432 | tf_op jit(solution)/shard_map/all_to_all | solution.py:336
  126.3 2.2 %finish_1.1 = f32[2,64,768]{2,1,0:T(8,128)} custom-call(s32[1]{0:T(128)} %bitcast.me_ref, bf16[16,400,128]{2,1,0:T(8,128)(2,1)} %all-to-all-done.got_ref, bf16[2,1024,768]{2,1,0:T(8,128)(2,1)S(1)} %copy-done, f32[2,64,768]{2,1,0:T(8,128)} %finish_0.1.rest_0_), custom_call_target="tpu_custom_call", output_to_operand_aliasing={{}: (3, {})} | custom-call | tf_op jit(solution)/shard_map/finish_1/pallas_call | solution.py:278
  (14 shorter events, 0.0 us)
Async XLA Ops:
  0.0 1.9 %copy-start.11 = (bf16[2048,768]{1,0:T(8,128)(2,1)S(1)}, bf16[2048,768]{1,0:T(8,128)(2,1)}, u32[]{:S(2)}) copy-start(bf16[2048,768]{1,0:T(8,128)(2,1)} %refs_0_.10) | copy-start | bytes 9437188
  1.9 0.7 copy-start.16
  2.6 6.0 %copy-start.12 = (bf16[2048,768]{1,0:T(8,128)(2,1)S(1)}, bf16[2048,768]{1,0:T(8,128)(2,1)}, u32[]{:S(2)}) copy-start(bf16[2048,768]{1,0:T(8,128)(2,1)} %refs_0_.10) | copy-start | bytes 9437188
  4.9 12.8 %collective-permute-start.7 = (bf16[256,768]{1,0:T(8,128)(2,1)S(1)}, bf16[256,768]{1,0:T(8,128)(2,1)S(1)}, u32[]{:S(2)}, u32[]{:S(2)}) collective-permute-start(bf16[256,768]{1,0:T(8,128)(2,1)S(1)} %get-tuple-element.67), channel_id=1, source_target_pairs={{0,32},{16,48},{32,64},{48,80},{64,96},{80,112},{96,0},{112,16},{1... | collective-permute-start | bytes 1179656 | tf_op jit(solution)/shard_map/ppermute | solution.py:305
  7.1 18.5 %collective-permute-start.8 = (bf16[256,768]{1,0:T(8,128)(2,1)S(1)}, bf16[256,768]{1,0:T(8,128)(2,1)S(1)}, u32[]{:S(2)}, u32[]{:S(2)}) collective-permute-start(bf16[256,768]{1,0:T(8,128)(2,1)S(1)} %get-tuple-element.68), channel_id=1, source_target_pairs={{0,96},{16,112},{32,0},{48,16},{64,32},{80,48},{96,64},{112,80},{1... | collective-permute-start | bytes 1179656 | tf_op jit(solution)/shard_map/ppermute | solution.py:305
  13.6 15.1 %collective-permute-start.4 = (bf16[256,768]{1,0:T(8,128)(2,1)S(1)}, bf16[256,768]{1,0:T(8,128)(2,1)S(1)}, u32[]{:S(2)}, u32[]{:S(2)}) collective-permute-start(bf16[256,768]{1,0:T(8,128)(2,1)S(1)} %get-tuple-element.63), channel_id=1, source_target_pairs={{0,48},{16,32},{32,80},{48,64},{64,112},{80,96},{96,16},{112,0},{1... | collective-permute-start | bytes 1179656 | tf_op jit(solution)/shard_map/ppermute | solution.py:305
  14.8 16.0 %collective-permute-start.5 = (bf16[256,768]{1,0:T(8,128)(2,1)S(1)}, bf16[256,768]{1,0:T(8,128)(2,1)S(1)}, u32[]{:S(2)}, u32[]{:S(2)}) collective-permute-start(bf16[256,768]{1,0:T(8,128)(2,1)S(1)} %get-tuple-element.64), channel_id=1, source_target_pairs={{0,112},{16,96},{32,16},{48,0},{64,48},{80,32},{96,80},{112,64},{1... | collective-permute-start | bytes 1179656 | tf_op jit(solution)/shard_map/ppermute | solution.py:305
  16.7 14.2 %collective-permute-start.6 = (bf16[256,768]{1,0:T(8,128)(2,1)S(1)}, bf16[256,768]{1,0:T(8,128)(2,1)S(1)}, u32[]{:S(2)}, u32[]{:S(2)}) collective-permute-start(bf16[256,768]{1,0:T(8,128)(2,1)S(1)} %get-tuple-element.65), channel_id=1, source_target_pairs={{0,16},{16,0},{32,48},{48,32},{64,80},{80,64},{96,112},{112,96},{1... | collective-permute-start | bytes 1179656 | tf_op jit(solution)/shard_map/ppermute | solution.py:305
  17.7 17.9 %collective-permute-start.2 = (bf16[256,768]{1,0:T(8,128)(2,1)S(1)}, bf16[256,768]{1,0:T(8,128)(2,1)S(1)}, u32[]{:S(2)}, u32[]{:S(2)}) collective-permute-start(bf16[256,768]{1,0:T(8,128)(2,1)S(1)} %get-tuple-element.61), channel_id=1, source_target_pairs={{0,64},{16,80},{32,96},{48,112},{64,0},{80,16},{96,32},{112,48},{1... | collective-permute-start | bytes 1179656 | tf_op jit(solution)/shard_map/ppermute | solution.py:305
  22.1 21.9 %copy-start = (bf16[2,1024,768]{2,1,0:T(8,128)(2,1)S(1)}, bf16[2,1024,768]{2,1,0:T(8,128)(2,1)}, u32[]{:S(2)}) copy-start(bf16[2,1024,768]{2,1,0:T(8,128)(2,1)} %cents_ref.5) | copy-start | bytes 9437188
  25.5 23.9 %copy-start.13 = (bf16[256,768]{1,0:T(8,128)(2,1)}, bf16[256,768]{1,0:T(8,128)(2,1)S(1)}, u32[]{:S(2)}) copy-start(bf16[256,768]{1,0:T(8,128)(2,1)S(1)} %get-tuple-element.58) | copy-start | bytes 1179652
  25.5 23.9 %copy-start.14 = (bf16[256,768]{1,0:T(8,128)(2,1)}, bf16[256,768]{1,0:T(8,128)(2,1)S(1)}, u32[]{:S(2)}) copy-start(bf16[256,768]{1,0:T(8,128)(2,1)S(1)} %get-tuple-element.57) | copy-start | bytes 1179652
  25.5 23.9 %copy-start.15 = (bf16[256,768]{1,0:T(8,128)(2,1)}, bf16[256,768]{1,0:T(8,128)(2,1)S(1)}, u32[]{:S(2)}) copy-start(bf16[256,768]{1,0:T(8,128)(2,1)S(1)} %get-tuple-element.81) | copy-start | bytes 1179652
  25.6 27.9 %collective-permute-start.3 = (bf16[256,768]{1,0:T(8,128)(2,1)S(1)}, bf16[256,768]{1,0:T(8,128)(2,1)S(1)}, u32[]{:S(2)}, u32[]{:S(2)}) collective-permute-start(bf16[256,768]{1,0:T(8,128)(2,1)S(1)} %get-tuple-element.62), channel_id=1, source_target_pairs={{0,80},{16,64},{32,112},{48,96},{64,16},{80,0},{96,48},{112,32},{1... | collective-permute-start | bytes 1179656 | tf_op jit(solution)/shard_map/ppermute | solution.py:305
  28.7 28.5 %collective-permute-start.10 = (bf16[256,768]{1,0:T(8,128)(2,1)S(1)}, bf16[256,768]{1,0:T(8,128)(2,1)S(1)}, u32[]{:S(2)}, u32[]{:S(2)}) collective-permute-start(bf16[256,768]{1,0:T(8,128)(2,1)S(1)} %get-tuple-element.74), channel_id=1, source_target_pairs={{0,96},{16,112},{32,0},{48,16},{64,32},{80,48},{96,64},{112,80},{1... | collective-permute-start | bytes 1179656 | tf_op jit(solution)/shard_map/ppermute | solution.py:305
  30.8 27.1 %collective-permute-start.11 = (bf16[256,768]{1,0:T(8,128)(2,1)S(1)}, bf16[256,768]{1,0:T(8,128)(2,1)S(1)}, u32[]{:S(2)}, u32[]{:S(2)}) collective-permute-start(bf16[256,768]{1,0:T(8,128)(2,1)S(1)} %get-tuple-element.75), channel_id=1, source_target_pairs={{0,48},{16,32},{32,80},{48,64},{64,112},{80,96},{96,16},{112,0},{1... | collective-permute-start | bytes 1179656 | tf_op jit(solution)/shard_map/ppermute | solution.py:305
  30.8 29.3 %collective-permute-start.12 = (bf16[256,768]{1,0:T(8,128)(2,1)S(1)}, bf16[256,768]{1,0:T(8,128)(2,1)S(1)}, u32[]{:S(2)}, u32[]{:S(2)}) collective-permute-start(bf16[256,768]{1,0:T(8,128)(2,1)S(1)} %get-tuple-element.76), channel_id=1, source_target_pairs={{0,112},{16,96},{32,16},{48,0},{64,48},{80,32},{96,80},{112,64},{1... | collective-permute-start | bytes 1179656 | tf_op jit(solution)/shard_map/ppermute | solution.py:305
  35.5 25.6 %collective-permute-start.9 = (bf16[256,768]{1,0:T(8,128)(2,1)S(1)}, bf16[256,768]{1,0:T(8,128)(2,1)S(1)}, u32[]{:S(2)}, u32[]{:S(2)}) collective-permute-start(bf16[256,768]{1,0:T(8,128)(2,1)S(1)} %get-tuple-element.73), channel_id=1, source_target_pairs={{0,32},{16,48},{32,64},{48,80},{64,96},{80,112},{96,0},{112,16},{1... | collective-permute-start | bytes 1179656 | tf_op jit(solution)/shard_map/ppermute | solution.py:305
  44.6 0.8 copy-start.1
  57.2 0.8 copy-start.3
  57.9 0.8 copy-start.5
  60.1 0.8 copy-start.7
  61.2 0.8 copy-start.9
  61.9 33.8 %all-to-all-start.1 = ((bf16[16,400,128]{2,1,0:T(8,128)(2,1)}), bf16[16,400,128]{2,1,0:T(8,128)(2,1)}, u32[]{:S(2)}, u32[]{:S(2)}) async-start(bf16[16,400,128]{2,1,0:T(8,128)(2,1)} %last_0.1), calls=%async_computation.1 | async-start | bytes 3276800 | tf_op jit(solution)/shard_map/all_to_all | solution.py:336
  69.6 4.2 %collective-permute-start.13 = (bf16[256,768]{1,0:T(8,128)(2,1)}, bf16[256,768]{1,0:T(8,128)(2,1)S(1)}, u32[]{:S(2)}, u32[]{:S(2)}) collective-permute-start(bf16[256,768]{1,0:T(8,128)(2,1)} %copy-done.15), channel_id=1, source_target_pairs={{0,16},{16,0},{32,48},{48,32},{64,80},{80,64},{96,112},{112,96},{1... | collective-permute-start | bytes 1179656 | tf_op jit(solution)/shard_map/ppermute | solution.py:305
  70.6 14.0 %collective-permute-start = (bf16[256,768]{1,0:T(8,128)(2,1)}, bf16[256,768]{1,0:T(8,128)(2,1)S(1)}, u32[]{:S(2)}, u32[]{:S(2)}) collective-permute-start(bf16[256,768]{1,0:T(8,128)(2,1)} %copy-done.14), channel_id=1, source_target_pairs={{0,64},{16,80},{32,96},{48,112},{64,0},{80,16},{96,32},{112,48},{1... | collective-permute-start | bytes 1179656 | tf_op jit(solution)/shard_map/ppermute | solution.py:305
  72.9 19.1 %collective-permute-start.1 = (bf16[256,768]{1,0:T(8,128)(2,1)}, bf16[256,768]{1,0:T(8,128)(2,1)S(1)}, u32[]{:S(2)}, u32[]{:S(2)}) collective-permute-start(bf16[256,768]{1,0:T(8,128)(2,1)} %copy-done.13), channel_id=1, source_target_pairs={{0,80},{16,64},{32,112},{48,96},{64,16},{80,0},{96,48},{112,32},{1... | collective-permute-start | bytes 1179656 | tf_op jit(solution)/shard_map/ppermute | solution.py:305
  73.8 1.0 copy-start.2
  74.9 1.0 copy-start.4
  75.9 1.0 copy-start.6
  76.9 1.0 copy-start.8
  77.9 1.0 copy-start.10
  95.8 30.5 %all-to-all-start = ((bf16[16,400,128]{2,1,0:T(8,128)(2,1)}), bf16[16,400,128]{2,1,0:T(8,128)(2,1)}, u32[]{:S(2)}, u32[]{:S(2)}) async-start(bf16[16,400,128]{2,1,0:T(8,128)(2,1)} %last_1.1), calls=%async_computation | async-start | bytes 3276800 | tf_op jit(solution)/shard_map/all_to_all | solution.py:336

commit v2 on v1

--- a/solution.py
+++ b/solution.py
@@ -16,9 +16,9 @@
 PAD_TEST = 32.0
 TAIL_ROWS = 16
 PIECES = 4
-HOPS = ((1, 0), (3, 0), (1, 1), (3, 1), (2, 0), (2, 1), (0, 1), (0, 0))
-STAGES = (((7, 0, 1), (2, 3, 6), (4, 5)), ((7, 0, 1, 2, 3, 6), (4, 5)))
-TIED = 4
+HOPS = ((2, 0), (2, 1), (1, 0), (3, 0), (1, 1), (3, 1), (0, 1), (0, 0))
+STAGES = (((7, 0, 1), (2, 3, 6), (4, 5)), ((7, 0, 1), (2, 3, 6), (4, 5)))
+TIED = 2
 FIRST = 2
 VMEM = pl.BlockSpec(memory_space=pltpu.VMEM)
 SMEM = pl.BlockSpec(memory_space=pltpu.SMEM)
@@ -73,12 +73,12 @@
     made = [jax.ShapeDtypeStruct((cap, width), jnp.bfloat16)] * blocks
     kept = [jax.ShapeDtypeStruct((lists, count), jnp.int32), jax.ShapeDtypeStruct((lists, LANES), jnp.int32)]
     first = keys is None
-    operands = [ids, rows] if first else [rows, *keys]
+    operands = [ids, pltpu.with_memory_space_constraint(rows, pltpu.HBM)] if first else [rows, *keys]
     made = (kept if first else []) + made
     out = pl.pallas_call(
         functools.partial(pack_kernel, first, hops, index, local),
         out_shape=made,
-        in_specs=[VMEM, pl.BlockSpec(memory_space=pl.ANY)] if first else [VMEM] * len(operands),
+        in_specs=[VMEM, pl.BlockSpec(memory_space=pltpu.HBM)] if first else [VMEM] * len(operands),
         out_specs=[VMEM] * len(made),
         scratch_shapes=[pltpu.VMEM((count, width), jnp.bfloat16), pltpu.SemaphoreType.DMA] if first else [],
         compiler_params=PARAMS,
@@ -317,8 +317,8 @@
     keys, sent = pack(HOPS[:FIRST], 0, local, embeddings, lists, cap, ids=ids)
     sent += pack(HOPS[FIRST:], 0, local, embeddings, lists, cap, keys=keys)
     later = []
-    for at in range(0, groups, TIED):
-        later += pack(HOPS[at : at + TIED], 1, local, embeddings, lists, cap, keys=keys)
+    for at in range(0, groups, 4):
+        later += pack(HOPS[at : at + 4], 1, local, embeddings, lists, cap, keys=keys)
     sent[-1], later = tie((sent[-1], later))
     norm = norms(centroids)
     rows = [[hop(b, step, groups) for b, step in zip(blocks, HOPS)] for blocks in (sent, later)]

time: 130 us -> 127 us (0.977)
  starting transfers between devices: 43.7 us -> 34.8 us
  waiting for transfers between devices: 32.8 us -> 40.6 us
  local copies, waits for them, and re-layouts: 11.5 us -> 6.91 us
  Pallas kernels: 40.3 us -> 44.1 us
    ppermute x14, starting transfers between devices: 29.6 us -> 20.5 us  [hop(): lax.ppermute(block, 'list', [(g, target(g, step, groups)) for g in range(...]
    ppermute x14, waiting for transfers between devices: 11 us -> 18.5 us  [hop(): lax.ppermute(block, 'list', [(g, target(g, step, groups)) for g in range(...]
    unnamed x34 -> x28, local copies, waits for them, and re-layouts: 11.5 us -> 6.91 us
    pallas_call x3 -> x4, Pallas kernels: 13.6 us -> 15.9 us  [stats(): pl.pallas_call(functools.partial(stats_kernel, index, len(rows), carried...]
    pallas_call x4, Pallas kernels: 14.1 us -> 15.7 us  [pack(): pl.pallas_call(functools.partial(pack_kernel, first, hops, index, local),...]
  transfers between devices with their start and end apart: 16 -> 16, of which waited for: 5 -> 5; matrix products, arithmetic and copies ran while one was open for 0% -> 0% of each run, Pallas kernels for 28% -> 30%
where the time goes in v2:
time: 127 us
  Pallas kernels  44.1 us (35%)
  waiting for transfers between devices  40.6 us (32%)
  starting transfers between devices  34.8 us (27%)
  local copies, waits for them, and re-layouts  6.91 us (5%)
    all_to_all x2, waiting for transfers between devices, per_device(): lax.all_to_all(part, 'shard', split_axis=0, concat_axis=0, tiled=True)  22.1 us
    ppermute x14, starting transfers between devices, hop(): lax.ppermute(block, 'list', [(g, target(g, step, groups)) for g in range(...  20.5 us
    ppermute x14, waiting for transfers between devices, hop(): lax.ppermute(block, 'list', [(g, target(g, step, groups)) for g in range(...  18.5 us
    pallas_call x4, Pallas kernels, stats(): pl.pallas_call(functools.partial(stats_kernel, index, len(rows), carried...  15.9 us
    pallas_call x4, Pallas kernels, pack(): pl.pallas_call(functools.partial(pack_kernel, first, hops, index, local),...  15.7 us
    all_to_all x2, starting transfers between devices, per_device(): lax.all_to_all(part, 'shard', split_axis=0, concat_axis=0, tiled=True)  14.3 us
    pallas_call x2, Pallas kernels, last_stats(): pl.pallas_call(functools.partial(last_kernel, index, len(rows), shares),...  7.46 us
    unnamed x28, local copies, waits for them, and re-layouts  6.91 us
  transfers between devices with their start and end apart: 16, of which 5 were waited for; matrix products, arithmetic and copies ran while one was open for 0% of the time, Pallas kernels for 30%

profile of v2, /device:TPU:1, one launch (start us, length us, event | category | flops | bytes accessed | tf_op | source)
XLA Modules:
  0.0 126.8 jit_solution(14561195629046584429)
XLA Ops:
  0.0 0.8 copy-done.13
  0.8 3.8 %pack.4 = (s32[16,2048]{1,0:T(8,128)S(1)}, s32[16,128]{1,0:T(8,128)S(1)}, bf16[256,768]{1,0:T(8,128)(2,1)S(1)}, bf16[256,768]{1,0:T(8,128)(2,1)S(1)}) custom-call(s32[1,2048]{1,0:T(1,128)S(1)} %bitcast.2, bf16[2048,768]{1,0:T(8,128)(2,1)} %refs_0_.11), custom_call_target="tpu_custom_call" | custom-call | flops 1610612736 | bytes 3145728 | tf_op jit(solution)/shard_map/pack/pallas_call | solution.py:78
  4.7 3.8 %collective-permute-start.10 = (bf16[256,768]{1,0:T(8,128)(2,1)S(1)}, bf16[256,768]{1,0:T(8,128)(2,1)S(1)}, u32[]{:S(2)}, u32[]{:S(2)}) collective-permute-start(bf16[256,768]{1,0:T(8,128)(2,1)S(1)} %get-tuple-element.70), channel_id=1, source_target_pairs={{0,64},{16,80},{32,96},{48,112},{64,0},{80,16},{96,32},{112,48},{1... | collective-permute-start | bytes 1179656 | tf_op jit(solution)/shard_map/ppermute | solution.py:305
  8.5 0.8 collective-permute-start.11
  9.3 0.0 copy-done.7
  9.3 5.0 %pack.5 = (bf16[256,768]{1,0:T(8,128)(2,1)S(1)}, bf16[256,768]{1,0:T(8,128)(2,1)S(1)}, bf16[256,768]{1,0:T(8,128)(2,1)S(1)}, bf16[256,768]{1,0:T(8,128)(2,1)S(1)...) custom-call(bf16[2048,768]{1,0:T(8,128)(2,1)S(1)} %copy-done.7, s32[16,2048]{1,0:T(8,128)S(1)} %get-tuple-element.46.refs_1_, ...), custom_call_target="tpu_custom_call" | custom-call | flops 4831838208 | bytes 3145728 | tf_op jit(solution)/shard_map/pack/pallas_call | solution.py:78
  14.3 1.4 %collective-permute-start.7 = (bf16[256,768]{1,0:T(8,128)(2,1)S(1)}, bf16[256,768]{1,0:T(8,128)(2,1)S(1)}, u32[]{:S(2)}, u32[]{:S(2)}) collective-permute-start(bf16[256,768]{1,0:T(8,128)(2,1)S(1)} %get-tuple-element.66), channel_id=1, source_target_pairs={{0,32},{16,48},{32,64},{48,80},{64,96},{80,112},{96,0},{112,16},{1... | collective-permute-start | bytes 1179656 | tf_op jit(solution)/shard_map/ppermute | solution.py:305
  15.8 1.5 %collective-permute-start.8 = (bf16[256,768]{1,0:T(8,128)(2,1)S(1)}, bf16[256,768]{1,0:T(8,128)(2,1)S(1)}, u32[]{:S(2)}, u32[]{:S(2)}) collective-permute-start(bf16[256,768]{1,0:T(8,128)(2,1)S(1)} %get-tuple-element.67), channel_id=1, source_target_pairs={{0,96},{16,112},{32,0},{48,16},{64,32},{80,48},{96,64},{112,80},{1... | collective-permute-start | bytes 1179656 | tf_op jit(solution)/shard_map/ppermute | solution.py:305
  17.3 0.5 collective-permute-start.9
  17.8 3.4 %pack.6 = (bf16[256,768]{1,0:T(8,128)(2,1)S(1)}, bf16[256,768]{1,0:T(8,128)(2,1)S(1)}, bf16[256,768]{1,0:T(8,128)(2,1)S(1)}, bf16[256,768]{1,0:T(8,128)(2,1)S(1)}) custom-call(bf16[2048,768]{1,0:T(8,128)(2,1)S(1)} %copy-done.7, s32[16,2048]{1,0:T(8,128)S(1)} %get-tuple-element.46.refs_1_, s32[16,128]{1,0:T(8,128)S(1)} %get-tuple-element.47.refs_2_), custom_call_target="tpu_custom_call" | custom-call | flops 3221225472 | bytes 3145728 | tf_op jit(solution)/shard_map/pack/pallas_call | solution.py:78
  21.2 0.0 copy-start.11
  21.2 0.8 copy-done.11
  22.0 0.8 copy-done.12
  22.8 3.4 %pack.7 = (bf16[256,768]{1,0:T(8,128)(2,1)S(1)}, bf16[256,768]{1,0:T(8,128)(2,1)S(1)}, bf16[256,768]{1,0:T(8,128)(2,1)S(1)}, bf16[256,768]{1,0:T(8,128)(2,1)S(1)}) custom-call(bf16[2048,768]{1,0:T(8,128)(2,1)S(1)} %copy-done.7, s32[16,2048]{1,0:T(8,128)S(1)} %get-tuple-element.46.refs_1_, s32[16,128]{1,0:T(8,128)S(1)} %get-tuple-element.47.refs_2_), custom_call_target="tpu_custom_call" | custom-call | flops 3221225472 | bytes 3145728 | tf_op jit(solution)/shard_map/pack/pallas_call | solution.py:78
  26.2 0.0 copy-start.8
  26.2 0.0 copy-start.9
  26.2 0.0 copy-start.10
  26.2 0.0 collective-permute-done.10.refs_3_
  26.2 0.1 collective-permute-start.5
  26.3 1.1 collective-permute-done.11.refs_4_
  27.4 1.8 %collective-permute-start.6 = (bf16[256,768]{1,0:T(8,128)(2,1)S(1)}, bf16[256,768]{1,0:T(8,128)(2,1)S(1)}, u32[]{:S(2)}, u32[]{:S(2)}) collective-permute-start(bf16[256,768]{1,0:T(8,128)(2,1)S(1)} %get-tuple-element.65), channel_id=1, source_target_pairs={{0,112},{16,96},{32,16},{48,0},{64,48},{80,32},{96,80},{112,64},{1... | collective-permute-start | bytes 1179656 | tf_op jit(solution)/shard_map/ppermute | solution.py:305
  29.3 5.7 %collective-permute-done.7.refs_2_ = bf16[256,768]{1,0:T(8,128)(2,1)S(1)} collective-permute-done((bf16[256,768]{1,0:T(8,128)(2,1)S(1)}, bf16[256,768]{1,0:T(8,128)(2,1)S(1)}, u32[]{:S(2)}, u32[]{:S(2)}) %collective-permute-start.7) | collective-permute-done | bytes 393248 | tf_op jit(solution)/shard_map/ppermute | solution.py:305
  35.0 3.0 %collective-permute-start.12 = (bf16[256,768]{1,0:T(8,128)(2,1)S(1)}, bf16[256,768]{1,0:T(8,128)(2,1)S(1)}, u32[]{:S(2)}, u32[]{:S(2)}) collective-permute-start(bf16[256,768]{1,0:T(8,128)(2,1)S(1)} %get-tuple-element.76), channel_id=1, source_target_pairs={{0,64},{16,80},{32,96},{48,112},{64,0},{80,16},{96,32},{112,48},{1... | collective-permute-start | bytes 1179656 | tf_op jit(solution)/shard_map/ppermute | solution.py:305
  38.0 0.0 collective-permute-done.8.refs_3_
  38.0 1.0 collective-permute-start.13
  39.0 0.0 copy-done
  39.0 0.7 norms.1
  39.7 4.0 %stats_0.2 = (f32[1024,768]{1,0:T(8,128)S(1)}, f32[1024,128]{1,0:T(8,128)S(1)}) custom-call(bf16[2,1024,768]{2,1,0:T(8,128)(2,1)S(1)} %copy-done, f32[1024,128]{1,0:T(8,128)S(1)} %get-tuple-element.63.refs_1_, bf16[256,768]{1,0:T(8,128)(2,1)S(1)} %get-tuple-element.69.refs_2_, bf16[256,768]{1,0:T(8,128)(2,1)S(1)} %collective-permute-done.10.refs_3_, ...), custom_call_target="tpu_custom_call" | custom-call | tf_op jit(solution)/shard_map/stats_0/pallas_call | solution.py:204
  43.7 0.0 copy-done.8
  43.7 0.0 copy-done.9
  43.7 0.0 copy-done.10
  43.7 0.0 collective-permute-done.9.refs_4_
  43.7 4.0 %stats_0.3 = (f32[1024,768]{1,0:T(8,128)S(1)}, f32[1024,128]{1,0:T(8,128)S(1)}) custom-call(bf16[2,1024,768]{2,1,0:T(8,128)(2,1)S(1)} %copy-done, f32[1024,128]{1,0:T(8,128)S(1)} %get-tuple-element.63.refs_1_, bf16[256,768]{1,0:T(8,128)(2,1)S(1)} %collective-permute-done.7.refs_2_, bf16[256,768]{1,0:T(8,128)(2,1)S(1)} %collective-permute-done.8.refs_3_, ...), custom_call_target="tpu_custom_call" | custom-call | tf_op jit(solution)/shard_map/stats_0/pallas_call | solution.py:204
  47.7 0.0 copy-done.1
  47.7 0.0 collective-permute-done.5.refs_2_
  47.7 0.0 collective-permute-done.6.refs_3_
  47.7 3.7 %last_0.1 = bf16[16,400,128]{2,1,0:T(8,128)(2,1)} custom-call(bf16[2,1024,768]{2,1,0:T(8,128)(2,1)S(1)} %copy-done, f32[1024,128]{1,0:T(8,128)S(1)} %get-tuple-element.63.refs_1_, bf16[256,768]{1,0:T(8,128)(2,1)S(1)} %collective-permute-done.5.refs_2_, bf16[256,768]{1,0:T(8,128)(2,1)S(1)} %collective-permute-done.6.refs_3_, ...), custom_call_target="tpu_custom_call" | custom-call | tf_op jit(solution)/shard_map/last_0/pallas_call | solution.py:220
  51.4 0.0 collective-permute-done.12.refs_3_
  51.5 0.0 copy-start.3
  51.5 0.7 copy-done.3
  52.2 7.8 %collective-permute-done.13.refs_4_ = bf16[256,768]{1,0:T(8,128)(2,1)S(1)} collective-permute-done((bf16[256,768]{1,0:T(8,128)(2,1)S(1)}, bf16[256,768]{1,0:T(8,128)(2,1)S(1)}, u32[]{:S(2)}, u32[]{:S(2)}) %collective-permute-start.13) | collective-permute-done | bytes 393248 | tf_op jit(solution)/shard_map/ppermute | solution.py:305
  60.0 0.7 copy-done.5
  60.8 7.7 %all-to-all-start.1 = ((bf16[16,400,128]{2,1,0:T(8,128)(2,1)}), bf16[16,400,128]{2,1,0:T(8,128)(2,1)}, u32[]{:S(2)}, u32[]{:S(2)}) async-start(bf16[16,400,128]{2,1,0:T(8,128)(2,1)} %last_0.1), calls=%async_computation.1 | async-start | bytes 3276800 | tf_op jit(solution)/shard_map/all_to_all | solution.py:336
  68.5 1.4 %collective-permute-start.2 = (bf16[256,768]{1,0:T(8,128)(2,1)}, bf16[256,768]{1,0:T(8,128)(2,1)S(1)}, u32[]{:S(2)}, u32[]{:S(2)}) collective-permute-start(bf16[256,768]{1,0:T(8,128)(2,1)} %copy-done.12), channel_id=1, source_target_pairs={{0,32},{16,48},{32,64},{48,80},{64,96},{80,112},{96,0},{112,16},{1... | collective-permute-start | bytes 1179656 | tf_op jit(solution)/shard_map/ppermute | solution.py:305
  69.8 1.5 %collective-permute-start.3 = (bf16[256,768]{1,0:T(8,128)(2,1)}, bf16[256,768]{1,0:T(8,128)(2,1)S(1)}, u32[]{:S(2)}, u32[]{:S(2)}) collective-permute-start(bf16[256,768]{1,0:T(8,128)(2,1)} %copy-done.11), channel_id=1, source_target_pairs={{0,96},{16,112},{32,0},{48,16},{64,32},{80,48},{96,64},{112,80},{1... | collective-permute-start | bytes 1179656 | tf_op jit(solution)/shard_map/ppermute | solution.py:305
  71.4 0.6 collective-permute-start.4
  72.0 0.0 collective-permute-start
  72.0 3.0 %collective-permute-start.1 = (bf16[256,768]{1,0:T(8,128)(2,1)}, bf16[256,768]{1,0:T(8,128)(2,1)S(1)}, u32[]{:S(2)}, u32[]{:S(2)}) collective-permute-start(bf16[256,768]{1,0:T(8,128)(2,1)} %copy-done.8), channel_id=1, source_target_pairs={{0,112},{16,96},{32,16},{48,0},{64,48},{80,32},{96,80},{112,64},{1... | collective-permute-start | bytes 1179656 | tf_op jit(solution)/shard_map/ppermute | solution.py:305
  74.9 1.0 copy-done.2
  76.0 1.0 copy-done.4
  77.0 1.0 copy-done.6
  78.0 4.0 %stats_1.2 = (f32[1024,768]{1,0:T(8,128)S(1)}, f32[1024,128]{1,0:T(8,128)S(1)}) custom-call(bf16[2,1024,768]{2,1,0:T(8,128)(2,1)S(1)} %copy-done, f32[1024,128]{1,0:T(8,128)S(1)} %copy-done.2, bf16[256,768]{1,0:T(8,128)(2,1)S(1)} %get-tuple-element.62.refs_2_, bf16[256,768]{1,0:T(8,128)(2,1)S(1)} %copy-done.4, bf16[256,768]{1,0:T(8,128)(2,1)S(1)} %copy-done.6), custom_call_target="tpu_custom_call" | custom-call | tf_op jit(solution)/shard_map/stats_1/pallas_call | solution.py:204
  81.9 0.0 collective-permute-done.2.refs_2_
  81.9 0.0 collective-permute-done.3.refs_3_
  81.9 0.0 collective-permute-done.4.refs_4_
  82.0 4.0 %stats_1.3 = (f32[1024,768]{1,0:T(8,128)S(1)}, f32[1024,128]{1,0:T(8,128)S(1)}) custom-call(bf16[2,1024,768]{2,1,0:T(8,128)(2,1)S(1)} %copy-done, f32[1024,128]{1,0:T(8,128)S(1)} %copy-done.2, bf16[256,768]{1,0:T(8,128)(2,1)S(1)} %collective-permute-done.2.refs_2_, bf16[256,768]{1,0:T(8,128)(2,1)S(1)} %collective-permute-done.3.refs_3_, ...), custom_call_target="tpu_custom_call" | custom-call | tf_op jit(solution)/shard_map/stats_1/pallas_call | solution.py:204
  85.9 3.8 %collective-permute-done.refs_2_ = bf16[256,768]{1,0:T(8,128)(2,1)S(1)} collective-permute-done((bf16[256,768]{1,0:T(8,128)(2,1)}, bf16[256,768]{1,0:T(8,128)(2,1)S(1)}, u32[]{:S(2)}, u32[]{:S(2)}) %collective-permute-start) | collective-permute-done | bytes 393248 | tf_op jit(solution)/shard_map/ppermute | solution.py:305
  89.7 0.0 collective-permute-done.1.refs_3_
  89.7 3.7 %last_1.1 = bf16[16,400,128]{2,1,0:T(8,128)(2,1)} custom-call(bf16[2,1024,768]{2,1,0:T(8,128)(2,1)S(1)} %copy-done, f32[1024,128]{1,0:T(8,128)S(1)} %copy-done.2, bf16[256,768]{1,0:T(8,128)(2,1)S(1)} %collective-permute-done.refs_2_, bf16[256,768]{1,0:T(8,128)(2,1)S(1)} %collective-permute-done.1.refs_3_, f32[1024,768]{1,0:T(8,128)S(1)} %get-tuple-element.82.refs_4_, ...), custom_call_target="tpu_custom_call" | custom-call | tf_op jit(solution)/shard_map/last_1/pallas_call | solution.py:220
  93.5 0.0 all-to-all-done.1.got_ref
  93.5 6.6 %all-to-all-start = ((bf16[16,400,128]{2,1,0:T(8,128)(2,1)}), bf16[16,400,128]{2,1,0:T(8,128)(2,1)}, u32[]{:S(2)}, u32[]{:S(2)}) async-start(bf16[16,400,128]{2,1,0:T(8,128)(2,1)} %last_1.1), calls=%async_computation | async-start | bytes 3276800 | tf_op jit(solution)/shard_map/all_to_all | solution.py:336
  100.1 2.2 %finish_0.1.rest_0_ = f32[2,64,768]{2,1,0:T(8,128)} custom-call(s32[1]{0:T(128)} %bitcast.me_ref, bf16[16,400,128]{2,1,0:T(8,128)(2,1)} %all-to-all-done.1.got_ref, bf16[2,1024,768]{2,1,0:T(8,128)(2,1)S(1)} %copy-done), custom_call_target="tpu_custom_call" | custom-call | tf_op jit(solution)/shard_map/finish_0/pallas_call | solution.py:278
  102.3 22.1 %all-to-all-done.got_ref = bf16[16,400,128]{2,1,0:T(8,128)(2,1)} async-done(((bf16[16,400,128]{2,1,0:T(8,128)(2,1)}), bf16[16,400,128]{2,1,0:T(8,128)(2,1)}, u32[]{:S(2)}, u32[]{:S(2)}) %all-to-all-start) | async-done | bytes 1638432 | tf_op jit(solution)/shard_map/all_to_all | solution.py:336
  124.4 2.2 %finish_1.1 = f32[2,64,768]{2,1,0:T(8,128)} custom-call(s32[1]{0:T(128)} %bitcast.me_ref, bf16[16,400,128]{2,1,0:T(8,128)(2,1)} %all-to-all-done.got_ref, bf16[2,1024,768]{2,1,0:T(8,128)(2,1)S(1)} %copy-done, f32[2,64,768]{2,1,0:T(8,128)} %finish_0.1.rest_0_), custom_call_target="tpu_custom_call", output_to_operand_aliasing={{}: (3, {})} | custom-call | tf_op jit(solution)/shard_map/finish_1/pallas_call | solution.py:278
  (9 shorter events, 0.0 us)
Async XLA Ops:
  0.0 9.3 %copy-start.7 = (bf16[2048,768]{1,0:T(8,128)(2,1)S(1)}, bf16[2048,768]{1,0:T(8,128)(2,1)}, u32[]{:S(2)}) copy-start(bf16[2048,768]{1,0:T(8,128)(2,1)} %refs_0_.11) | copy-start | bytes 9437188
  0.0 0.8 copy-start.13
  4.7 21.6 %collective-permute-start.10 = (bf16[256,768]{1,0:T(8,128)(2,1)S(1)}, bf16[256,768]{1,0:T(8,128)(2,1)S(1)}, u32[]{:S(2)}, u32[]{:S(2)}) collective-permute-start(bf16[256,768]{1,0:T(8,128)(2,1)S(1)} %get-tuple-element.70), channel_id=1, source_target_pairs={{0,64},{16,80},{32,96},{48,112},{64,0},{80,16},{96,32},{112,48},{1... | collective-permute-start | bytes 1179656 | tf_op jit(solution)/shard_map/ppermute | solution.py:305
  8.5 19.0 %collective-permute-start.11 = (bf16[256,768]{1,0:T(8,128)(2,1)S(1)}, bf16[256,768]{1,0:T(8,128)(2,1)S(1)}, u32[]{:S(2)}, u32[]{:S(2)}) collective-permute-start(bf16[256,768]{1,0:T(8,128)(2,1)S(1)} %get-tuple-element.71), channel_id=1, source_target_pairs={{0,80},{16,64},{32,112},{48,96},{64,16},{80,0},{96,48},{112,32},{1... | collective-permute-start | bytes 1179656 | tf_op jit(solution)/shard_map/ppermute | solution.py:305
  14.3 20.6 %collective-permute-start.7 = (bf16[256,768]{1,0:T(8,128)(2,1)S(1)}, bf16[256,768]{1,0:T(8,128)(2,1)S(1)}, u32[]{:S(2)}, u32[]{:S(2)}) collective-permute-start(bf16[256,768]{1,0:T(8,128)(2,1)S(1)} %get-tuple-element.66), channel_id=1, source_target_pairs={{0,32},{16,48},{32,64},{48,80},{64,96},{80,112},{96,0},{112,16},{1... | collective-permute-start | bytes 1179656 | tf_op jit(solution)/shard_map/ppermute | solution.py:305
  15.8 22.2 %collective-permute-start.8 = (bf16[256,768]{1,0:T(8,128)(2,1)S(1)}, bf16[256,768]{1,0:T(8,128)(2,1)S(1)}, u32[]{:S(2)}, u32[]{:S(2)}) collective-permute-start(bf16[256,768]{1,0:T(8,128)(2,1)S(1)} %get-tuple-element.67), channel_id=1, source_target_pairs={{0,96},{16,112},{32,0},{48,16},{64,32},{80,48},{96,64},{112,80},{1... | collective-permute-start | bytes 1179656 | tf_op jit(solution)/shard_map/ppermute | solution.py:305
  17.3 26.4 %collective-permute-start.9 = (bf16[256,768]{1,0:T(8,128)(2,1)S(1)}, bf16[256,768]{1,0:T(8,128)(2,1)S(1)}, u32[]{:S(2)}, u32[]{:S(2)}) collective-permute-start(bf16[256,768]{1,0:T(8,128)(2,1)S(1)} %get-tuple-element.68), channel_id=1, source_target_pairs={{0,16},{16,0},{32,48},{48,32},{64,80},{80,64},{96,112},{112,96},{1... | collective-permute-start | bytes 1179656 | tf_op jit(solution)/shard_map/ppermute | solution.py:305
  21.2 0.8 copy-start.11
  22.0 0.8 copy-start.12
  22.8 16.2 %copy-start = (bf16[2,1024,768]{2,1,0:T(8,128)(2,1)S(1)}, bf16[2,1024,768]{2,1,0:T(8,128)(2,1)}, u32[]{:S(2)}) copy-start(bf16[2,1024,768]{2,1,0:T(8,128)(2,1)} %cents_ref.5) | copy-start | bytes 9437188
  26.2 17.5 %copy-start.8 = (bf16[256,768]{1,0:T(8,128)(2,1)}, bf16[256,768]{1,0:T(8,128)(2,1)S(1)}, u32[]{:S(2)}) copy-start(bf16[256,768]{1,0:T(8,128)(2,1)S(1)} %get-tuple-element.58) | copy-start | bytes 1179652
  26.2 17.5 %copy-start.9 = (bf16[256,768]{1,0:T(8,128)(2,1)}, bf16[256,768]{1,0:T(8,128)(2,1)S(1)}, u32[]{:S(2)}) copy-start(bf16[256,768]{1,0:T(8,128)(2,1)S(1)} %get-tuple-element.57) | copy-start | bytes 1179652
  26.2 17.5 %copy-start.10 = (bf16[256,768]{1,0:T(8,128)(2,1)}, bf16[256,768]{1,0:T(8,128)(2,1)S(1)}, u32[]{:S(2)}) copy-start(bf16[256,768]{1,0:T(8,128)(2,1)S(1)} %get-tuple-element.61) | copy-start | bytes 1179652
  26.2 21.5 %collective-permute-start.5 = (bf16[256,768]{1,0:T(8,128)(2,1)S(1)}, bf16[256,768]{1,0:T(8,128)(2,1)S(1)}, u32[]{:S(2)}, u32[]{:S(2)}) collective-permute-start(bf16[256,768]{1,0:T(8,128)(2,1)S(1)} %get-tuple-element.64), channel_id=1, source_target_pairs={{0,48},{16,32},{32,80},{48,64},{64,112},{80,96},{96,16},{112,0},{1... | collective-permute-start | bytes 1179656 | tf_op jit(solution)/shard_map/ppermute | solution.py:305
  27.4 20.3 %collective-permute-start.6 = (bf16[256,768]{1,0:T(8,128)(2,1)S(1)}, bf16[256,768]{1,0:T(8,128)(2,1)S(1)}, u32[]{:S(2)}, u32[]{:S(2)}) collective-permute-start(bf16[256,768]{1,0:T(8,128)(2,1)S(1)} %get-tuple-element.65), channel_id=1, source_target_pairs={{0,112},{16,96},{32,16},{48,0},{64,48},{80,32},{96,80},{112,64},{1... | collective-permute-start | bytes 1179656 | tf_op jit(solution)/shard_map/ppermute | solution.py:305
  35.0 16.5 %collective-permute-start.12 = (bf16[256,768]{1,0:T(8,128)(2,1)S(1)}, bf16[256,768]{1,0:T(8,128)(2,1)S(1)}, u32[]{:S(2)}, u32[]{:S(2)}) collective-permute-start(bf16[256,768]{1,0:T(8,128)(2,1)S(1)} %get-tuple-element.76), channel_id=1, source_target_pairs={{0,64},{16,80},{32,96},{48,112},{64,0},{80,16},{96,32},{112,48},{1... | collective-permute-start | bytes 1179656 | tf_op jit(solution)/shard_map/ppermute | solution.py:305
  38.0 22.1 %collective-permute-start.13 = (bf16[256,768]{1,0:T(8,128)(2,1)S(1)}, bf16[256,768]{1,0:T(8,128)(2,1)S(1)}, u32[]{:S(2)}, u32[]{:S(2)}) collective-permute-start(bf16[256,768]{1,0:T(8,128)(2,1)S(1)} %get-tuple-element.77), channel_id=1, source_target_pairs={{0,80},{16,64},{32,112},{48,96},{64,16},{80,0},{96,48},{112,32},{1... | collective-permute-start | bytes 1179656 | tf_op jit(solution)/shard_map/ppermute | solution.py:305
  39.7 8.0 %copy-start.1 = (f32[1024,128]{1,0:T(8,128)}, f32[1024,128]{1,0:T(8,128)S(1)}, u32[]{:S(2)}) copy-start(f32[1024,128]{1,0:T(8,128)S(1)} %get-tuple-element.45.refs_1_) | copy-start | bytes 1572868
  51.5 0.7 copy-start.3
  60.0 0.7 copy-start.5
  60.8 32.7 %all-to-all-start.1 = ((bf16[16,400,128]{2,1,0:T(8,128)(2,1)}), bf16[16,400,128]{2,1,0:T(8,128)(2,1)}, u32[]{:S(2)}, u32[]{:S(2)}) async-start(bf16[16,400,128]{2,1,0:T(8,128)(2,1)} %last_0.1), calls=%async_computation.1 | async-start | bytes 3276800 | tf_op jit(solution)/shard_map/all_to_all | solution.py:336
  68.5 13.5 %collective-permute-start.2 = (bf16[256,768]{1,0:T(8,128)(2,1)}, bf16[256,768]{1,0:T(8,128)(2,1)S(1)}, u32[]{:S(2)}, u32[]{:S(2)}) collective-permute-start(bf16[256,768]{1,0:T(8,128)(2,1)} %copy-done.12), channel_id=1, source_target_pairs={{0,32},{16,48},{32,64},{48,80},{64,96},{80,112},{96,0},{112,16},{1... | collective-permute-start | bytes 1179656 | tf_op jit(solution)/shard_map/ppermute | solution.py:305
  69.8 12.1 %collective-permute-start.3 = (bf16[256,768]{1,0:T(8,128)(2,1)}, bf16[256,768]{1,0:T(8,128)(2,1)S(1)}, u32[]{:S(2)}, u32[]{:S(2)}) collective-permute-start(bf16[256,768]{1,0:T(8,128)(2,1)} %copy-done.11), channel_id=1, source_target_pairs={{0,96},{16,112},{32,0},{48,16},{64,32},{80,48},{96,64},{112,80},{1... | collective-permute-start | bytes 1179656 | tf_op jit(solution)/shard_map/ppermute | solution.py:305
  71.4 10.6 %collective-permute-start.4 = (bf16[256,768]{1,0:T(8,128)(2,1)}, bf16[256,768]{1,0:T(8,128)(2,1)S(1)}, u32[]{:S(2)}, u32[]{:S(2)}) collective-permute-start(bf16[256,768]{1,0:T(8,128)(2,1)} %copy-done.10), channel_id=1, source_target_pairs={{0,16},{16,0},{32,48},{48,32},{64,80},{80,64},{96,112},{112,96},{1... | collective-permute-start | bytes 1179656 | tf_op jit(solution)/shard_map/ppermute | solution.py:305
  72.0 17.7 %collective-permute-start = (bf16[256,768]{1,0:T(8,128)(2,1)}, bf16[256,768]{1,0:T(8,128)(2,1)S(1)}, u32[]{:S(2)}, u32[]{:S(2)}) collective-permute-start(bf16[256,768]{1,0:T(8,128)(2,1)} %copy-done.9), channel_id=1, source_target_pairs={{0,48},{16,32},{32,80},{48,64},{64,112},{80,96},{96,16},{112,0},{1... | collective-permute-start | bytes 1179656 | tf_op jit(solution)/shard_map/ppermute | solution.py:305
  72.0 17.8 %collective-permute-start.1 = (bf16[256,768]{1,0:T(8,128)(2,1)}, bf16[256,768]{1,0:T(8,128)(2,1)S(1)}, u32[]{:S(2)}, u32[]{:S(2)}) collective-permute-start(bf16[256,768]{1,0:T(8,128)(2,1)} %copy-done.8), channel_id=1, source_target_pairs={{0,112},{16,96},{32,16},{48,0},{64,48},{80,32},{96,80},{112,64},{1... | collective-permute-start | bytes 1179656 | tf_op jit(solution)/shard_map/ppermute | solution.py:305
  74.9 1.0 copy-start.2
  76.0 1.0 copy-start.4
  77.0 1.0 copy-start.6
  93.5 30.9 %all-to-all-start = ((bf16[16,400,128]{2,1,0:T(8,128)(2,1)}), bf16[16,400,128]{2,1,0:T(8,128)(2,1)}, u32[]{:S(2)}, u32[]{:S(2)}) async-start(bf16[16,400,128]{2,1,0:T(8,128)(2,1)} %last_1.1), calls=%async_computation | async-start | bytes 3276800 | tf_op jit(solution)/shard_map/all_to_all | solution.py:336
